TPU v7x, 128 devices: a whole 4x4x4 slice. The times are simulated.
128 devices in a mesh: dp: 16 (over y, x_hi, core), trow: 4 (over z), tcol: 2 (over x_lo).
Axes of the slice: x: 4 (x_hi: 2, x_lo: 2; x = x_hi * 2 + x_lo), y: 4, z: 4, core: 2. Of those that a mesh axis runs over, the one named last changes fastest.
Arguments:
- tokens: bfloat16 [16384, 2560], P(('dp', 'trow'), 'tcol'), may hold values from -6 to 6
- gate_weight: bfloat16 [6912, 2560], P(('trow', 'dp'), 'tcol'), may hold values from -0.125 to 0.125
- up_weight: bfloat16 [6912, 2560], P(('trow', 'dp'), 'tcol'), may hold values from -0.125 to 0.125
- cotangent: bfloat16 [16384, 6912], P('dp', 'trow'), may hold values from -6 to 6
Outputs:
- hidden: bfloat16 [16384, 6912], P('dp', 'trow')
- token_grad: bfloat16 [16384, 2560], P(('dp', 'trow'), 'tcol')
- gate_grad: float32 [6912, 2560], P(('trow', 'dp'), 'tcol')
- up_grad: float32 [6912, 2560], P(('trow', 'dp'), 'tcol')
All inputs are finite; a program needn't handle non-finite values.
Results may differ from a plain program's by a relative error of at most 0.0049.
Values may be sent and summed in bfloat16 or wider, within the bound.
A program may use at most 128 MiB of HBM per device.

v0:
```python
import jax
import jax.numpy as jnp
from jax import lax
from jax.sharding import PartitionSpec as P


def activate(gate_pre, up_pre, upstream):
    hidden = (jax.nn.silu(gate_pre) * up_pre).astype(jnp.bfloat16)
    back = upstream.astype(jnp.float32)
    sigmoid_gate = jax.nn.sigmoid(gate_pre)
    gate_delta = (back * up_pre * sigmoid_gate * (1.0 + gate_pre * (1.0 - sigmoid_gate))).astype(
        jnp.bfloat16
    )
    up_delta = (back * (gate_pre * sigmoid_gate)).astype(jnp.bfloat16)
    return (hidden, gate_delta, up_delta)


def times_rows(left, right):
    return lax.dot_general(
        left, right, (((1,), (1,)), ((), ())), preferred_element_type=jnp.float32
    )


def over_tokens(left, right):
    return lax.dot_general(
        left, right, (((0,), (0,)), ((), ())), preferred_element_type=jnp.float32
    )


def per_device(tokens, gate_weight, up_weight, cotangent):
    gathered = lax.all_gather(tokens, "trow", axis=0, tiled=True)
    gate_tile, up_tile = (
        lax.all_gather(gate_weight, "dp", axis=0, tiled=True),
        lax.all_gather(up_weight, "dp", axis=0, tiled=True),
    )
    gate_part = times_rows(gathered, gate_tile)
    up_part = times_rows(gathered, up_tile)
    gate_pre, up_pre = lax.psum((gate_part, up_part), "tcol")
    hidden, gate_delta, up_delta = activate(gate_pre, up_pre, cotangent)
    token_term = jnp.dot(gate_delta, gate_tile, preferred_element_type=jnp.float32) + jnp.dot(
        up_delta, up_tile, preferred_element_type=jnp.float32
    )
    token_grad = lax.psum_scatter(token_term, "trow", scatter_dimension=0, tiled=True).astype(
        jnp.bfloat16
    )
    gate_term = over_tokens(gate_delta, gathered)
    up_term = over_tokens(up_delta, gathered)
    gate_total, up_total = (
        lax.psum_scatter(gate_term, "dp", scatter_dimension=0, tiled=True),
        lax.psum_scatter(up_term, "dp", scatter_dimension=0, tiled=True),
    )
    grad_scale = 1.0 / (gathered.shape[0] * lax.axis_size("dp")) ** 0.5
    return (hidden, token_grad, gate_total * grad_scale, up_total * grad_scale)


def solution(mesh):
    in_specs = (
        P(("dp", "trow"), "tcol"),
        P(("trow", "dp"), "tcol"),
        P(("trow", "dp"), "tcol"),
        P("dp", "trow"),
    )
    out_specs = (
        P("dp", "trow"),
        P(("dp", "trow"), "tcol"),
        P(("trow", "dp"), "tcol"),
        P(("trow", "dp"), "tcol"),
    )
    return jax.shard_map(
        per_device, mesh=mesh, in_specs=in_specs, out_specs=out_specs, check_vma=False
    )
```

profile of v0, /device:TPU:0, one launch (start us, length us, event | category | flops | bytes accessed | tf_op | source)
XLA Modules:
  0.0 765.2 jit_solution(6515318130610980676)
XLA Ops:
  7.2 0.0 all-gather.8.cloned.1.call-start
  7.2 0.7 all-gather.8.cloned.1.call-update
  7.9 0.0 all-gather.10.cloned.1.call-start
  7.9 0.7 all-gather.10.cloned.1.call-update
  8.6 0.0 all-gather.6.cloned.1.call-start
  8.7 0.7 all-gather.6.cloned.1.call-update
  9.4 0.0 all-reduce.8.cloned.1.call-start
  9.4 60.2 %all-gather.8.cloned.1.call-done = bf16[16,108,1280]{2,1,0:T(8,128)(2,1)} async-done(((bf16[1,108,1280]{2,1,0:T(8,128)(2,1)}), bf16[16,108,1280]{2,1,0:T(8,128)(2,1)}) %all-gather.8.cloned.1.call-update) | async-done | bytes 4423696 | tf_op jit(solution)/shard_map/all_gather | solution.py:33
  69.7 7.1 reshape.9
  76.7 50.0 %all-gather.10.cloned.1.call-done = bf16[16,108,1280]{2,1,0:T(8,128)(2,1)} async-done(((bf16[1,108,1280]{2,1,0:T(8,128)(2,1)}), bf16[16,108,1280]{2,1,0:T(8,128)(2,1)}) %all-gather.10.cloned.1.call-update) | async-done | bytes 4423696 | tf_op jit(solution)/shard_map/all_gather | solution.py:34
  126.7 7.1 reshape.11
  133.8 27.9 %all-gather.6.cloned.1.call-done = bf16[1024,1280]{1,0:T(8,128)(2,1)} async-done(((bf16[256,1280]{1,0:T(8,128)(2,1)}), bf16[1024,1280]{1,0:T(8,128)(2,1)}) %all-gather.6.cloned.1.call-update) | async-done | bytes 2621456 | tf_op jit(solution)/shard_map/all_gather | solution.py:31
  161.7 10.9 %fusion.8 = f32[1024,1728]{0,1:T(8,128)} fusion(bf16[1024,1280]{1,0:T(8,128)(2,1)} %all-gather.6.cloned.1.call-done, bf16[1728,1280]{1,0:T(8,128)(2,1)} %reshape.9), kind=kOutput, calls=%fused_computation.12 | convolution fusion | flops 4529848320 | bytes 14123008 | tf_op jit(solution)/shard_map/dot_general | solution.py:19
  172.6 6.7 fusion.9
  179.4 0.2 reduce-scatter.6.cloned.1.call-start
  179.6 329.0 %all-reduce.8.cloned.1.call-done = (f32[1024,1728]{0,1:T(8,128)}, f32[1024,1728]{0,1:T(8,128)}) async-done(((f32[1024,1728]{0,1:T(8,128)}, f32[1024,1728]{0,1:T(8,128)}), (f32[1024,1728]{0,1:T(8,128)}, f32[1024,1728]{0,1:T(8,128)})) %all-reduce.8.cloned.1.call-update) | async-done | bytes 14155792 | tf_op jit(solution)/shard_map/psum | solution.py:38
  508.7 9.7 %fusion.4 = (bf16[1024,1728]{0,1:T(8,128)(2,1)S(1)}, bf16[1024,1728]{0,1:T(8,128)(2,1)}, bf16[1024,1728]{0,1:T(8,128)(2,1)S(1)}) fusion(f32[1024,1728]{0,1:T(8,128)} %get-tuple-element.4, bf16[1024,1728]{0,1:T(8,128)(2,1)} %param.7, f32[1024,1728]{0,1:T(8,128)} %get-tuple-element.5), kind=kLoop, calls=%fused_computation.4 | loop fusion | flops 28311552 | bytes 28311552 | tf_op jit(solution)/shard_map/convert_element_type | solution.py:11
  518.4 10.1 %fusion.10 = f32[1024,1280]{1,0:T(8,128)S(1)} fusion(bf16[1024,1728]{0,1:T(8,128)(2,1)S(1)} %get-tuple-element.10, bf16[1728,1280]{1,0:T(8,128)(2,1)} %reshape.9), kind=kOutput, calls=%fused_computation.14 | convolution fusion | flops 4529848320 | bytes 13205504 | tf_op jit(solution)/shard_map/dot_general | solution.py:40
  528.6 7.0 convolution_add_fusion
  535.6 0.0 reduce-scatter.6.cloned.1.call-update
  535.6 2.0 copy-done.4
  537.6 9.2 %fusion.11 = f32[1728,1280]{1,0:T(8,128)} fusion(bf16[1024,1728]{0,1:T(8,128)(2,1)S(1)} %copy-done.4, bf16[1024,1280]{1,0:T(8,128)(2,1)} %all-gather.6.cloned.1.call-done), kind=kOutput, calls=%fused_computation.15 | convolution fusion | flops 4529848320 | bytes 15007744 | tf_op jit(solution)/shard_map/dot_general | solution.py:25
  546.8 7.0 fusion.12
  553.8 194.2 %fusion.7 = (f32[112,1280]{1,0:T(8,128)S(1)}, f32[112,1280]{1,0:T(8,128)S(1)}) fusion(f32[1728,1280]{1,0:T(8,128)} %fusion.11, f32[1728,1280]{1,0:T(8,128)} %fusion.12), kind=kCustom, calls=%all-reduce-scatter.2 | all-reduce-scatter fusion | flops 4587521 | bytes 18842112
  748.0 1.3 collective-permute-start.1
  749.4 3.2 collective-permute-start
  752.6 0.6 dynamic-slice.6
  753.8 0.4 concatenate.1
  754.3 0.4 concatenate
  754.7 0.9 dynamic-slice_multiply_fusion
  755.6 0.9 dynamic-slice_multiply_fusion.1
  756.4 2.2 convert_element_type.19
  (26 shorter events, 0.1 us)
Async XLA Ops:
  7.2 62.5 %all-gather.8.cloned.1.call-start = ((), (), s32[]{:S(2)}) async-start(), calls=%async_computation.3 | async-start | bytes 4874240 | tf_op jit(solution)/shard_map/all_gather | solution.py:33
  7.9 118.8 %all-gather.10.cloned.1.call-start = ((), (), s32[]{:S(2)}) async-start(), calls=%async_computation.4 | async-start | bytes 4874240 | tf_op jit(solution)/shard_map/all_gather | solution.py:34
  8.6 153.1 %all-gather.6.cloned.1.call-start = ((), (), s32[]{:S(2)}) async-start(), calls=%async_computation.1 | async-start | bytes 3276800 | tf_op jit(solution)/shard_map/all_gather | solution.py:31
  9.4 499.3 %all-reduce.8.cloned.1.call-start = ((), (), s32[]{:S(2)}) async-start(), calls=%async_computation.5 | async-start | bytes 28311552 | tf_op jit(solution)/shard_map/psum | solution.py:38
  161.7 10.9 %copy-start = (bf16[1728,1280]{1,0:T(8,128)(2,1)S(1)}, bf16[1728,1280]{1,0:T(8,128)(2,1)}, u32[]{:S(2)}) copy-start(bf16[1728,1280]{1,0:T(8,128)(2,1)} %reshape.11) | copy-start | bytes 13271044
  161.7 10.9 %copy-start.6 = (bf16[1024,1280]{1,0:T(8,128)(2,1)S(1)}, bf16[1024,1280]{1,0:T(8,128)(2,1)}, u32[]{:S(2)}) copy-start(bf16[1024,1280]{1,0:T(8,128)(2,1)} %all-gather.6.cloned.1.call-done) | copy-start | bytes 7864324
  179.4 349.2 %slice-start = ((s8[4423680]{0:T(1024)(128)(4,1)}), s8[229376]{0:T(1024)(128)(4,1)S(1)}, s32[]{:S(2)}) async-start(s8[4423680]{0:T(1024)(128)(4,1)} %bitcast.20), calls=%async_computation.6 | async-start | bytes 458752
  179.4 577.1 %reduce-scatter.6.cloned.1.call-start = ((), (), s32[]{:S(2)}) async-start(), calls=%async_computation.2 | async-start | bytes 6553600 | tf_op jit(solution)/shard_map/reduce_scatter | solution.py:43
  508.7 19.9 %slice-start.1 = ((s8[4423680]{0:T(1024)(128)(4,1)}), s8[4194304]{0:T(1024)(128)(4,1)S(1)}, s32[]{:S(2)}) async-start(s8[4423680]{0:T(1024)(128)(4,1)} %bitcast.20), calls=%async_computation.7 | async-start | bytes 8388608
  518.4 10.1 %copy-start.3 = (bf16[1024,1728]{0,1:T(8,128)(2,1)}, bf16[1024,1728]{0,1:T(8,128)(2,1)S(1)}, u32[]{:S(2)}) copy-start(bf16[1024,1728]{0,1:T(8,128)(2,1)S(1)} %get-tuple-element.10) | copy-start | bytes 10616836
  518.4 10.1 %copy-start.1 = (bf16[1024,1728]{0,1:T(8,128)(2,1)}, bf16[1024,1728]{0,1:T(8,128)(2,1)S(1)}, u32[]{:S(2)}) copy-start(bf16[1024,1728]{0,1:T(8,128)(2,1)S(1)} %get-tuple-element.12) | copy-start | bytes 10616836
  535.6 2.0 copy-start.4
  537.6 9.2 %copy-start.2 = (bf16[1024,1728]{0,1:T(8,128)(2,1)S(1)}, bf16[1024,1728]{0,1:T(8,128)(2,1)}, u32[]{:S(2)}) copy-start(bf16[1024,1728]{0,1:T(8,128)(2,1)} %copy-done.1) | copy-start | bytes 10616836
  537.6 9.2 %copy-start.7 = (bf16[1024,1280]{1,0:T(8,128)(2,1)S(1)}, bf16[1024,1280]{1,0:T(8,128)(2,1)}, u32[]{:S(2)}) copy-start(bf16[1024,1280]{1,0:T(8,128)(2,1)} %all-gather.6.cloned.1.call-done) | copy-start | bytes 7864324
  553.8 198.8 %copy-start.5 = (u32[128]{0:T(128)S(1)}, u32[128]{0:T(128)}, u32[]{:S(2)}) copy-start(u32[128]{0:T(128)} %constant.10) | copy-start | bytes 1540
  748.0 5.8 collective-permute-start.1
  749.4 4.9 collective-permute-start
Sparse Core Ops, SparseCore 0:
  10.5 59.1 all-gather.7
  72.1 54.5 all-gather.9
  128.4 33.2 all-gather.5
  179.5 329.1 all-reduce.7
  535.7 56.5 reduce-scatter.5
where the time goes:
time: 772 us; the launch traced here: 765 us
  waiting for transfers between devices  469 us (61%)
  blocking collectives  194 us (25%)
  matrix products  50.9 us (7%)
  local copies, waits for them, and re-layouts  17.7 us (2%)
  between operations  14.6 us (2%)
  other arithmetic  13.7 us (2%)
    psum x1, waiting for transfers between devices, per_device(): gate_pre, up_pre = lax.psum((gate_part, up_part), 'tcol')  329 us
    unnamed x1, blocking collectives  194 us
    all_gather x1, waiting for transfers between devices, per_device(): lax.all_gather(gate_weight, 'dp', axis=0, tiled=True)  60.2 us
    all_gather x1, waiting for transfers between devices, per_device(): lax.all_gather(up_weight, 'dp', axis=0, tiled=True)  50 us
    all_gather x1, waiting for transfers between devices, per_device(): gathered = lax.all_gather(tokens, 'trow', axis=0, tiled=True)  27.9 us
    unnamed x27, local copies, waits for them, and re-layouts  17.7 us
    dot_general x2, matrix products, times_rows(): lax.dot_general(left, right, (((1,), (1,)), ((), ())), preferred_element_...  17.6 us
    dot_general x2, matrix products, over_tokens(): lax.dot_general(left, right, (((0,), (0,)), ((), ())), preferred_element_...  16.2 us
  transfers between devices with their start and end apart: 7, of which 4 were waited for; matrix products, arithmetic and copies ran while one was open for 30% of the time, Pallas kernels for 0%

commit v1 on v0

v1 whole, which is shorter than its diff:
```python
import jax
import jax.numpy as jnp
from jax import lax
from jax.experimental import pallas as pl
from jax.experimental.pallas import tpu as pltpu
from jax.sharding import PartitionSpec as P

BF = jnp.bfloat16
F32 = jnp.float32
MESH = pl.DeviceIdType.MESH

SHARD = 108
SENT = 112
BLOCK = 128
HALF = 1280
CHUNK = 256
TOK = 1024
HID = 1024
TILE = 256
NT = HALF // TILE

T0, T1R, T1L, T2R, T2L, T3R, T3L = range(7)
WA, WB = 7, 8
W1R, W1L = 9, 11
W2R, W2L = 13, 14
WC = 15
HD = 23
G1R, G1L = 39, 41
G2R, G2L = 43, 45
GX = 47
CC = 48
Y1R, Y1L = 52, 53
Y2R, Y2L = 54, 55
XA, XB = 56, 57
N_SEM = 58


def ring(i):
    return i + i // 2 - 2 * (i // 3)


def rows_by_rows(left, right):
    return lax.dot_general(
        left, right, (((1,), (1,)), ((), ())), preferred_element_type=F32
    )


def kernel(
    tok_ref, w_ref, cot_ref,
    hid_out, tg_out, gr_out,
    tbuf, wbuf, dl, hid, dtr,
    tgs1, tgr1, tgs2, tgr2, tgo, txs, txr,
    cs, cr, own, y1s, y1r, y2s, y2r, xs, xr,
    ss, rs, ls,
):
    dp = lax.axis_index("dp")
    z = lax.axis_index("trow")
    l = lax.axis_index("tcol")
    k = dp % 2
    h = (dp // 2) % 2
    y = dp // 4

    def dev(y_, h_, k_, z_, l_):
        return {"dp": (y_ * 2 + h_) * 2 + k_, "trow": z_, "tcol": l_}

    zr, zl = (z + 1) % 4, (z + 3) % 4
    yr, yl = (y + 1) % 4, (y + 3) % 4
    z_right, z_left = dev(y, h, k, zr, l), dev(y, h, k, zl, l)
    y_right, y_left = dev(yr, h, k, z, l), dev(yl, h, k, z, l)
    core_peer = dev(y, h, 1 - k, z, l)
    x_peer = dev(y, h, k, z, 1 - l)
    swap_here = dev(y, h, l, z, k)
    swap_there = dev(y, 1 - h, l, z, k)
    on_self = k == l

    def remote(src, dst, at, to):
        return pltpu.make_async_remote_copy(
            src_ref=src, dst_ref=dst, send_sem=ss.at[at], recv_sem=rs.at[at],
            device_id=to, device_id_type=MESH,
        )

    barrier = pltpu.get_barrier_semaphore()
    for peer in (z_right, z_left, y_right, y_left, core_peer, x_peer, swap_there):
        pl.semaphore_signal(barrier, inc=1, device_id=peer, device_id_type=MESH)

    @pl.when(jnp.logical_not(on_self))
    def _():
        pl.semaphore_signal(barrier, inc=1, device_id=swap_here, device_id_type=MESH)
        pl.semaphore_wait(barrier, 8)

    @pl.when(on_self)
    def _():
        pl.semaphore_wait(barrier, 7)

    def tok_at(c, zz):
        return tbuf.at[c, pl.ds(pl.multiple_of(zz * CHUNK, CHUNK), CHUNK), :]

    def w_at(c, yy, hh):
        return wbuf.at[:, c, pl.ds(pl.multiple_of((yy * 2 + hh) * BLOCK, BLOCK), SENT), :]

    wa = remote(w_ref, w_at(l, y, h), WA, swap_here)
    wa_self = pltpu.make_async_copy(w_ref, w_at(l, y, h), ls.at[0])
    wb = remote(w_ref, w_at(l, y, h), WB, swap_there)

    @pl.when(on_self)
    def _():
        wa_self.start()

    @pl.when(jnp.logical_not(on_self))
    def _():
        wa.start()

    wb.start()
    t0 = remote(tok_ref, tok_at(l, z), T0, x_peer)
    t0.start()
    t1r = remote(tok_ref, tok_at(l, z), T1R, z_right)
    t1l = remote(tok_ref, tok_at(l, z), T1L, z_left)
    t1r.start()
    t1l.start()
    t_self = pltpu.make_async_copy(tok_ref, tok_at(l, z), ls.at[1])
    t_self.start()
    c_self = pltpu.make_async_copy(cot_ref, dl.at[0], ls.at[2])
    c_self.start()

    def clear(i, _):
        row = pl.ds(pl.multiple_of(i * BLOCK + SENT, 16), BLOCK - SENT)
        for m in range(2):
            for c in range(2):
                wbuf[m, c, row, :] = jnp.zeros((BLOCK - SENT, HALF), BF)
        return 0

    lax.fori_loop(0, 8, clear, 0)

    def piece(yy, hh):
        return w_at(k, yy, hh)

    def share(at, yy, hh):
        cp = remote(piece(yy, hh), piece(yy, hh), WC + at, core_peer)
        cp.start()
        return cp

    @pl.when(on_self)
    def _():
        wa_self.wait()

    @pl.when(jnp.logical_not(on_self))
    def _():
        wa.wait_recv()

    w1r_a = remote(piece(y, h), piece(y, h), W1R, y_right)
    w1l_a = remote(piece(y, h), piece(y, h), W1L, y_left)
    w1r_a.start()
    w1l_a.start()
    shares = [share(0, y, h)]
    wb.wait_recv()
    w1r_b = remote(piece(y, 1 - h), piece(y, 1 - h), W1R + 1, y_right)
    w1l_b = remote(piece(y, 1 - h), piece(y, 1 - h), W1L + 1, y_left)
    w1r_b.start()
    w1l_b.start()
    shares.append(share(1, y, 1 - h))
    t0.wait_recv()
    t2r = remote(tok_at(1 - l, z), tok_at(1 - l, z), T2R, z_right)
    t2l = remote(tok_at(1 - l, z), tok_at(1 - l, z), T2L, z_left)
    t2r.start()
    t2l.start()
    t1r.wait_recv()
    t3r = remote(tok_at(l, zl), tok_at(l, zl), T3R, z_right)
    t3r.start()
    w1r_a.wait_recv()
    w2r = remote(piece(yl, h), piece(yl, h), W2R, y_right)
    w2r.start()
    shares.append(share(2, yl, h))
    w1l_a.wait_recv()
    shares.append(share(3, yr, h))
    w1l_b.wait_recv()
    w2l = remote(piece(yr, 1 - h), piece(yr, 1 - h), W2L, y_left)
    w2l.start()
    shares.append(share(4, yr, 1 - h))
    w1r_b.wait_recv()
    shares.append(share(5, yl, 1 - h))
    t1l.wait_recv()
    t2l.wait_recv()
    t3l = remote(tok_at(1 - l, zr), tok_at(1 - l, zr), T3L, z_left)
    t3l.start()
    t2r.wait_recv()
    t_self.wait()
    c_self.wait()
    for at in range(6):
        shares[at].wait_recv()

    def hidden_copy(at, zz, yy):
        tile = hid.at[
            pl.ds(pl.multiple_of(zz * CHUNK, CHUNK), CHUNK),
            pl.ds(pl.multiple_of(yy * TILE, TILE), TILE),
        ]
        there = hid_out.at[
            l,
            pl.ds(pl.multiple_of(zz * CHUNK, CHUNK), CHUNK),
            pl.ds(pl.multiple_of(yy * TILE, TILE), TILE),
        ]
        return remote(tile, there, HD + at, x_peer)

    def activate(at, zi, yi):
        zz = (z + ring(zi)) % 4
        yy = (y + ring(yi)) % 4
        rows = pl.ds(pl.multiple_of(zz * CHUNK, CHUNK), CHUNK)
        cols = pl.ds(pl.multiple_of(yy * TILE, TILE), TILE)
        x0, x1 = tbuf[0, rows, :], tbuf[1, rows, :]
        gate = rows_by_rows(x0, wbuf[0, 0, cols, :]) + rows_by_rows(x1, wbuf[0, 1, cols, :])
        up = rows_by_rows(x0, wbuf[1, 0, cols, :]) + rows_by_rows(x1, wbuf[1, 1, cols, :])
        back = dl[0, rows, cols].astype(F32)
        s = jax.nn.sigmoid(gate)
        gs = gate * s
        hid[rows, cols] = (gs * up).astype(BF)
        dl[0, rows, cols] = (back * up * s * (1.0 + gate * (1.0 - s))).astype(BF)
        dl[1, rows, cols] = (back * gs).astype(BF)
        hidden_copy(at, zz, yy).start()

    def first_nine(i, _):
        activate(i, i % 3, i // 3)
        return 0

    lax.fori_loop(0, 9, first_nine, 0)
    w2r.wait_recv()
    shares.append(share(6, (y + 2) % 4, h))
    w2l.wait_recv()
    shares.append(share(7, (y + 2) % 4, 1 - h))
    t3r.wait_recv()
    t3l.wait_recv()

    def last_tokens(i, _):
        activate(9 + i, 3, i)
        return 0

    lax.fori_loop(0, 3, last_tokens, 0)
    shares[6].wait_recv()
    shares[7].wait_recv()

    def last_units(i, _):
        activate(12 + i, i, 3)
        return 0

    lax.fori_loop(0, 4, last_units, 0)
    h_self = pltpu.make_async_copy(hid, hid_out.at[l], ls.at[3])
    h_self.start()

    def tg_tiles(zz, o, put):
        c = (1 - l) if o == 0 else l
        rows = pl.ds(pl.multiple_of(zz * CHUNK, CHUNK), CHUNK)

        def step(n, _):
            cols = pl.ds(pl.multiple_of(n * TILE, TILE), TILE)
            out = jnp.dot(dl[0, rows, :], wbuf[0, c, :, cols], preferred_element_type=F32)
            out += jnp.dot(dl[1, rows, :], wbuf[1, c, :, cols], preferred_element_type=F32)
            put(out, cols)
            return 0

        lax.fori_loop(0, NT, step, 0)

    g1 = []
    for o in range(2):
        def put_far(out, cols, o=o):
            tgs1[o, :, cols] = out.astype(BF)

        tg_tiles((z + 2) % 4, o, put_far)
        g1r = remote(tgs1.at[o, pl.ds(0, 128), :], tgr1.at[0, o], G1R + o, z_right)
        g1l = remote(tgs1.at[o, pl.ds(128, 128), :], tgr1.at[1, o], G1L + o, z_left)
        g1r.start()
        g1l.start()
        g1.append((g1r, g1l))

    def gr_group(gi, yy, slot):
        for m in range(2):
            cols = pl.ds(pl.multiple_of(yy * TILE, TILE), TILE)
            dtr[m] = jnp.transpose(dl[m, :, cols])
        for mine in range(2):
            c = k if mine else 1 - k
            for m in range(2):

                def step(n, _, mine=mine, m=m, c=c):
                    cols = pl.ds(pl.multiple_of(n * TILE, TILE), TILE)
                    out = jnp.dot(dtr[m], tbuf[c, :, cols], preferred_element_type=F32)
                    for hh in range(2):
                        part = out[hh * BLOCK : hh * BLOCK + SENT]
                        if mine:
                            own[slot, hh, m, :, cols] = part
                        else:
                            cs[gi, hh, m, :, cols] = part.astype(BF)
                    return 0

                lax.fori_loop(0, NT, step, 0)
            if not mine:
                cp = remote(cs.at[gi], cr.at[gi], CC + gi, core_peer)
                cp.start()
        return cp

    cc = [gr_group(0, (y + 2) % 4, 0)]
    cc[0].wait_recv()
    y1 = []
    for hh, (at, to) in enumerate(((Y1R, y_right), (Y1L, y_left))):
        for m in range(2):
            y1s[hh, m] = (own[0, hh, m] + cr[0, hh, m].astype(F32)).astype(BF)
        cp = remote(y1s.at[hh], y1r.at[hh], at, to)
        cp.start()
        y1.append(cp)
    cc.append(gr_group(1, yr, 1))
    cc.append(gr_group(2, yl, 0))

    for o in range(2):
        def put_own(out, cols, o=o):
            tgo[o, :, cols] = out

        tg_tiles(z, o, put_own)

    g2 = []
    for o in range(2):
        for d, (zz, at, to) in enumerate(((zr, G2R, z_right), (zl, G2L, z_left))):
            g1[o][d].wait_recv()

            def put_near(out, cols, o=o, d=d):
                lo, hi = out[:128], out[128:]
                if d == 0:
                    lo = lo + tgr1[0, o, :, cols].astype(F32)
                else:
                    hi = hi + tgr1[1, o, :, cols].astype(F32)
                tgs2[d, o, pl.ds(0, 128), cols] = lo.astype(BF)
                tgs2[d, o, pl.ds(128, 128), cols] = hi.astype(BF)

            tg_tiles(zz, o, put_near)
            cp = remote(tgs2.at[d, o], tgr2.at[d, o], at + o, to)
            cp.start()
            g2.append(cp)

    y2 = []
    for d, (at, to) in enumerate(((Y2R, y_right), (Y2L, y_left))):
        cc[1 + d].wait_recv()
        y1[d].wait_recv()
        for hh in range(2):
            for m in range(2):
                part = own[1 - d, hh, m] + cr[1 + d, hh, m].astype(F32)
                if hh == d:
                    part = part + y1r[d, m].astype(F32)
                y2s[d, hh, m] = part.astype(BF)
        cp = remote(y2s.at[d], y2r.at[d], at, to)
        cp.start()
        y2.append(cp)

    cc.append(gr_group(3, y, 1))
    cc[3].wait_recv()

    g2[0].wait_recv()
    g2[1].wait_recv()
    txs[...] = (tgo[0] + tgr2[0, 0].astype(F32) + tgr2[1, 0].astype(F32)).astype(BF)
    gx = remote(txs, txr, GX, x_peer)
    gx.start()
    y2[0].wait_recv()
    y2[1].wait_recv()
    for hh in range(2):
        for m in range(2):
            part = own[1, hh, m] + cr[3, hh, m].astype(F32)
            part = part + y2r[0, hh, m].astype(F32) + y2r[1, hh, m].astype(F32)
            xs[hh, m] = part.astype(BF)
    xa = remote(xs.at[h], xr.at[0], XA, swap_here)
    xa_self = pltpu.make_async_copy(xs.at[h], xr.at[0], ls.at[4])
    xb = remote(xs.at[1 - h], xr.at[1], XB, swap_there)
    xb.start()

    @pl.when(on_self)
    def _():
        xa_self.start()

    @pl.when(jnp.logical_not(on_self))
    def _():
        xa.start()

    g2[2].wait_recv()
    g2[3].wait_recv()
    gx.wait_recv()
    tg_out[...] = (
        tgo[1] + tgr2[0, 1].astype(F32) + tgr2[1, 1].astype(F32) + txr[...].astype(F32)
    ).astype(BF)

    @pl.when(on_self)
    def _():
        xa_self.wait()

    @pl.when(jnp.logical_not(on_self))
    def _():
        xa.wait_recv()

    xb.wait_recv()
    scale = 1.0 / 128.0
    for m in range(2):
        gr_out[m] = (xr[0, m].astype(F32) + xr[1, m].astype(F32)) * scale

    def hidden_done(i, _):
        cp = hidden_copy(i, 0, 0)
        cp.wait_recv()
        cp.wait_send()
        return 0

    lax.fori_loop(0, 16, hidden_done, 0)
    h_self.wait()

    @pl.when(jnp.logical_not(on_self))
    def _():
        wa.wait_send()
        xa.wait_send()

    for cp in [wb, t0, t1r, t1l, t2r, t2l, t3r, t3l, w1r_a, w1l_a, w1r_b, w1l_b, w2r, w2l]:
        cp.wait_send()
    for cp in shares + cc + y1 + y2 + g2 + [gx, xb] + [c for pair in g1 for c in pair]:
        cp.wait_send()


def fused(tokens, weights, cot):
    vmem = pl.BlockSpec(memory_space=pltpu.VMEM)
    hbm = pl.BlockSpec(memory_space=pl.ANY)
    flops = 3 * 2 * 2 * TOK * HID * 2 * HALF
    return pl.pallas_call(
        kernel,
        out_shape=(
            jax.ShapeDtypeStruct((2, TOK, HID), BF),
            jax.ShapeDtypeStruct((CHUNK, HALF), BF),
            jax.ShapeDtypeStruct((2, SENT, HALF), F32),
        ),
        in_specs=[vmem, vmem, hbm],
        out_specs=(hbm, vmem, vmem),
        scratch_shapes=[
            pltpu.VMEM((2, TOK, HALF), BF),
            pltpu.VMEM((2, 2, HID, HALF), BF),
            pltpu.VMEM((2, TOK, HID), BF),
            pltpu.VMEM((TOK, HID), BF),
            pltpu.VMEM((2, TILE, TOK), BF),
            pltpu.VMEM((2, CHUNK, HALF), BF),
            pltpu.VMEM((2, 2, 128, HALF), BF),
            pltpu.VMEM((2, 2, CHUNK, HALF), BF),
            pltpu.VMEM((2, 2, CHUNK, HALF), BF),
            pltpu.VMEM((2, CHUNK, HALF), F32),
            pltpu.VMEM((CHUNK, HALF), BF),
            pltpu.VMEM((CHUNK, HALF), BF),
            pltpu.VMEM((4, 2, 2, SENT, HALF), BF),
            pltpu.VMEM((4, 2, 2, SENT, HALF), BF),
            pltpu.VMEM((2, 2, 2, SENT, HALF), F32),
            pltpu.VMEM((2, 2, SENT, HALF), BF),
            pltpu.VMEM((2, 2, SENT, HALF), BF),
            pltpu.VMEM((2, 2, 2, SENT, HALF), BF),
            pltpu.VMEM((2, 2, 2, SENT, HALF), BF),
            pltpu.VMEM((2, 2, SENT, HALF), BF),
            pltpu.VMEM((2, 2, SENT, HALF), BF),
            pltpu.SemaphoreType.DMA((N_SEM,)),
            pltpu.SemaphoreType.DMA((N_SEM,)),
            pltpu.SemaphoreType.DMA((5,)),
        ],
        compiler_params=pltpu.CompilerParams(
            collective_id=0, has_side_effects=True, vmem_limit_bytes=64 * 1024 * 1024,
        ),
        cost_estimate=pl.CostEstimate(
            flops=flops, bytes_accessed=16 * 1024 * 1024, transcendentals=TOK * HID
        ),
        name="swiglu_grid",
    )(tokens, weights, cot)


def per_device(tokens, gate_weight, up_weight, cotangent):
    l = lax.axis_index("tcol")
    weights = jnp.pad(jnp.stack([gate_weight, up_weight]), ((0, 0), (0, SENT - SHARD), (0, 0)))
    blocks = cotangent.reshape(TOK, 8, 2, SHARD)
    mine = lax.dynamic_index_in_dim(blocks, l, 2, keepdims=False)
    cot = jnp.pad(mine, ((0, 0), (0, 0), (0, BLOCK - SHARD))).reshape(TOK, HID)
    hid, token_grad, grads = fused(tokens, weights, cot)
    both = hid.reshape(2, TOK, 8, BLOCK)[..., :SHARD]
    hidden = jnp.transpose(both, (1, 2, 0, 3)).reshape(TOK, 16 * SHARD)
    return hidden, token_grad, grads[0, :SHARD], grads[1, :SHARD]


def solution(mesh):
    in_specs = (
        P(("dp", "trow"), "tcol"),
        P(("trow", "dp"), "tcol"),
        P(("trow", "dp"), "tcol"),
        P("dp", "trow"),
    )
    out_specs = (
        P("dp", "trow"),
        P(("dp", "trow"), "tcol"),
        P(("trow", "dp"), "tcol"),
        P(("trow", "dp"), "tcol"),
    )
    return jax.shard_map(
        per_device, mesh=mesh, in_specs=in_specs, out_specs=out_specs, check_vma=False
    )
```

time: 772 us -> 193 us (0.25)
  waiting for transfers between devices: 469 us -> 0 us
  blocking collectives: 194 us -> 0 us
  Pallas kernels: 0 us -> 155 us
  matrix products: 50.9 us -> 0 us
  local copies, waits for them, and re-layouts: 17.7 us -> 32.6 us
  between operations: 14.6 us -> 0.67 us
  other arithmetic: 13.7 us -> 1.89 us
    psum x1 -> x0, waiting for transfers between devices: 329 us -> none  [per_device(): gate_pre, up_pre = lax.psum((gate_part, up_part), 'tcol')]
    unnamed x1 -> x0, blocking collectives: 194 us -> none
    pallas_call x0 -> x1, Pallas kernels: none -> 155 us  [fused(): pl.pallas_call(kernel, out_shape=(jax.ShapeDtypeStruct((2, TOK, HID), BF)...]
    all_gather x3 -> x0, waiting for transfers between devices: 138 us -> none  [the longest x1 60.2 us: per_device(): lax.all_gather(gate_weight, 'dp', axis=0, tiled=True)]
    dot_general x6 -> x0, matrix products: 50.9 us -> none  [the longest x2 17.6 us: times_rows(): lax.dot_general(left, right, (((1,), (1,)), ((), ())), preferred_element_...]
    convert_element_type x2 -> x0, other arithmetic: 12 us -> none  [the longest x1 9.74 us: activate(): (back * up_pre * sigmoid_gate * (1.0 + gate_pre * (1.0 - sigmoid_gate)))....]
    reshape x0 -> x2, local copies, waits for them, and re-layouts: none -> 9.27 us  [the longest x1 4.67 us: per_device(): hidden = jnp.transpose(both, (1, 2, 0, 3)).reshape(TOK, 16 * SHARD)]
    unnamed x27 -> x9, local copies, waits for them, and re-layouts: 17.7 us -> 18.9 us
  transfers between devices with their start and end apart: 7 -> 0, of which waited for: 4 -> 0; matrix products, arithmetic and copies ran while one was open for 30% -> 0% of each run, Pallas kernels for 0% -> 0%
where the time goes in v1:
time: 193 us; the launch traced here: 191 us
  Pallas kernels  155 us (80%)
  local copies, waits for them, and re-layouts  32.6 us (17%)
    pallas_call x1, Pallas kernels, fused(): pl.pallas_call(kernel, out_shape=(jax.ShapeDtypeStruct((2, TOK, HID), BF)...  155 us
    unnamed x9, local copies, waits for them, and re-layouts  18.9 us
    reshape x1, local copies, waits for them, and re-layouts, per_device(): hidden = jnp.transpose(both, (1, 2, 0, 3)).reshape(TOK, 16 * SHARD)  4.67 us
    reshape x1, local copies, waits for them, and re-layouts, per_device(): blocks = cotangent.reshape(TOK, 8, 2, SHARD)  4.6 us

profile of v1, /device:TPU:0, one launch (start us, length us, event | category | flops | bytes accessed | tf_op | source)
XLA Modules:
  0.0 190.5 jit_solution(645614438753625511)
XLA Ops:
  0.6 1.9 fusion.2.w_ref
  2.5 4.6 %reshape.20 = bf16[1024,8,2,108]{0,3,2,1:T(8,128)(2,1)} reshape(bf16[1024,1728]{0,1:T(8,128)(2,1)} %param.7) | data formatting | bytes 7077888 | tf_op jit(solution)/shard_map/reshape | solution.py:468
  7.1 2.9 %dynamic-slice_bitcast_fusion = bf16[1024,8,108]{0,2,1:T(8,128)(2,1)} fusion(bf16[1024,8,2,108]{0,3,2,1:T(8,128)(2,1)} %reshape.20, s32[]{:T(128)S(6)} %select_n.4), kind=kLoop, calls=%fused_computation.1 | loop fusion | bytes 3538948 | tf_op jit(solution)/shard_map/jit(dynamic_index_in_dim)/squeeze | solution.py:469
  10.0 3.4 %copy.15 = bf16[1024,8,108]{2,1,0:T(8,128)(2,1)S(1)} copy(bf16[1024,8,108]{0,2,1:T(8,128)(2,1)} %dynamic-slice_bitcast_fusion) | data formatting | bytes 3538944
  13.4 0.4 pad.9.clone
  13.8 1.9 %copy.20 = bf16[128,8,8,128]{3,1,2,0:T(8,128)(2,1)} copy(bf16[128,8,8,128]{3,2,1,0:T(8,128)(2,1)S(1)} %bitcast.25) | data formatting | bytes 4194304
  15.8 155.4 %swiglu_grid.1 = (bf16[2,1024,1024]{2,1,0:T(8,128)(2,1)}, bf16[256,1280]{1,0:T(8,128)(2,1)}, f32[2,112,1280]{2,1,0:T(8,128)}) custom-call(bf16[256,1280]{1,0:T(8,128)(2,1)} %tok_ref.1, bf16[2,112,1280]{2,1,0:T(8,128)(2,1)} %fusion.2.w_ref, bf16[1024,1024]{1,0:T(8,128)(2,1)} %bitcast.27), custom_call_target="tpu_custom_call" | custom-call | flops 32212254720 | bytes 16777216 | tf_op jit(solution)/shard_map/swiglu_grid/pallas_call | solution.py:420
  171.2 5.2 %copy.18 = bf16[256,8,8,128]{3,2,1,0:T(8,128)(2,1)} copy(bf16[256,8,8,128]{3,1,2,0:T(8,128)(2,1)} %bitcast.26) | data formatting | bytes 8388608
  176.4 7.2 %copy.14 = bf16[2,1024,8,108]{1,3,0,2:T(8,128)(2,1)} copy(bf16[2,1024,8,108]{3,2,1,0:T(8,128)(2,1)} %bitcast.23) | data formatting | bytes 7077888
  183.7 0.0 copy-start
  183.7 4.7 %reshape.23 = bf16[1024,1728]{0,1:T(8,128)(2,1)} reshape(bf16[1024,8,2,108]{0,3,2,1:T(8,128)(2,1)} %bitcast.24) | data formatting | bytes 7077888 | tf_op jit(solution)/shard_map/reshape | solution.py:473
  188.4 0.0 copy-done
  188.4 0.0 copy-start.1
  188.4 1.1 slice_bitcast_fusion
  189.4 0.3 copy-done.1
  189.7 0.8 copy.22
Async XLA Ops:
  183.7 4.7 %copy-start = (f32[2,112,1280]{2,1,0:T(8,128)S(1)}, f32[2,112,1280]{2,1,0:T(8,128)}, u32[]{:S(2)}) copy-start(f32[2,112,1280]{2,1,0:T(8,128)} %get-tuple-element.9) | copy-start | bytes 3440644
  188.4 1.3 copy-start.1

commit v2 on v0

v2 whole, which is shorter than its diff:
```python
import jax
import jax.numpy as jnp
from jax import lax
from jax.experimental import pallas as pl
from jax.experimental.pallas import tpu as pltpu
from jax.sharding import PartitionSpec as P

BF = jnp.bfloat16
F32 = jnp.float32
MESH = pl.DeviceIdType.MESH

SHARD = 108
SENT = 112
BLOCK = 128
HALF = 1280
CHUNK = 256
TOK = 1024
TILE = 256
PAIR = 2 * TILE
HID = 1024
COMPACT = 896
FF_TILE = 16 * SHARD

names = {}


def place(name, count=1):
    names[name] = sum(n for _, n in names.values()), count
    return names[name][0]


T0, T1R, T1L, T2R, T2L, T3R, T3L, T5 = [place("t%d" % i) for i in range(8)]
WA, WB = place("wa", 2), place("wb", 2)
W1RA, W1LA, W1RB, W1LB = [place("w1%d" % i, 2) for i in range(4)]
W2R, W2L = place("w2r", 2), place("w2l", 2)
WC = place("wc", 16)
HD = place("hd", 4)
G1R, G1L, G2R, G2L = [place("g%d" % i, 2) for i in range(4)]
GX = place("gx")
CC = place("cc", 4)
Y1R, Y1L = place("y1r"), place("y1l")
Y2R, Y2L = place("y2r", 2), place("y2l", 2)
XA, XB = place("xa"), place("xb")
N_SEM = sum(n for _, n in names.values())


def rows_by_rows(left, right):
    return lax.dot_general(
        left, right, (((1,), (1,)), ((), ())), preferred_element_type=F32
    )


def over_rows(left, right):
    return lax.dot_general(
        left, right, (((0,), (0,)), ((), ())), preferred_element_type=F32
    )


def at_rows(i, n=CHUNK):
    return pl.ds(pl.multiple_of(i * n, n), n)


def kernel(
    tok_ref, gw_ref, uw_ref, cot_ref,
    hid_out, tg_out, gr_out,
    tbuf, wbuf, wsrc, dl, hid, raw,
    tgs1, tgr1, tgs2, tgr2, tgo, txs, txr,
    cs, cr, own, y1s, y1r, y2s, y2r, xs, xr,
    ss, rs, ls,
):
    dp = lax.axis_index("dp")
    z = lax.axis_index("trow")
    l = lax.axis_index("tcol")
    k = dp % 2
    h = (dp // 2) % 2
    y = dp // 4

    def dev(y_, h_, k_, z_, l_):
        return {"dp": (y_ * 2 + h_) * 2 + k_, "trow": z_, "tcol": l_}

    zr, zl, zo = (z + 1) % 4, (z + 3) % 4, (z + 2) % 4
    yr, yl, yo = (y + 1) % 4, (y + 3) % 4, (y + 2) % 4
    z_right, z_left = dev(y, h, k, zr, l), dev(y, h, k, zl, l)
    y_right, y_left = dev(yr, h, k, z, l), dev(yl, h, k, z, l)
    core_peer = dev(y, h, 1 - k, z, l)
    x_peer = dev(y, h, k, z, 1 - l)
    swap_here = dev(y, h, l, z, k)
    swap_there = dev(y, 1 - h, l, z, k)
    on_self = k == l
    sent = []

    def remote(src, dst, at, to):
        return pltpu.make_async_remote_copy(
            src_ref=src, dst_ref=dst, send_sem=ss.at[at], recv_sem=rs.at[at],
            device_id=to, device_id_type=MESH,
        )

    def send(src, dst, at, to):
        cp = remote(src, dst, at, to)
        cp.start()
        sent.append(cp)
        return cp

    barrier = pltpu.get_barrier_semaphore()
    for peer in (z_right, z_left, y_right, y_left, core_peer, x_peer, swap_there):
        pl.semaphore_signal(barrier, inc=1, device_id=peer, device_id_type=MESH)

    @pl.when(jnp.logical_not(on_self))
    def _():
        pl.semaphore_signal(barrier, inc=1, device_id=swap_here, device_id_type=MESH)

    def raw_copy(i):
        slot = i % 2
        return pltpu.make_async_copy(
            cot_ref.at[at_rows(i), :], raw.at[slot], ls.at[2 + slot]
        )

    raw_copy(0).start()
    raw_copy(1).start()
    for m, ref in enumerate((gw_ref, uw_ref)):
        wsrc[m, pl.ds(96, 16), :] = jnp.zeros((16, HALF), BF)
        wsrc[m, pl.ds(0, SHARD), :] = ref[...]

    @pl.when(on_self)
    def _():
        pl.semaphore_wait(barrier, 7)

    @pl.when(jnp.logical_not(on_self))
    def _():
        pl.semaphore_wait(barrier, 8)

    def tok_at(c, zz):
        return tbuf.at[c, at_rows(zz), :]

    def tok_half(c, zz, part):
        return tbuf.at[c, pl.ds(pl.multiple_of(zz * CHUNK + part * 128, 128), 128), :]

    def w_at(c, yy, hh, m):
        return wbuf.at[c, yy, m, pl.ds(pl.multiple_of(hh * BLOCK, BLOCK), SENT), :]

    wa = [remote(wsrc.at[m], w_at(l, y, h, m), WA + m, swap_here) for m in range(2)]
    wa_self = pltpu.make_async_copy(
        wsrc, wbuf.at[l, y, :, pl.ds(pl.multiple_of(h * BLOCK, BLOCK), SENT), :], ls.at[0]
    )

    @pl.when(on_self)
    def _():
        wa_self.start()

    @pl.when(jnp.logical_not(on_self))
    def _():
        wa[0].start()
        wa[1].start()

    wb = [send(wsrc.at[m], w_at(l, y, h, m), WB + m, swap_there) for m in range(2)]
    t1r = send(tok_ref, tok_at(l, z), T1R, z_right)
    t1l = send(tok_ref, tok_at(l, z), T1L, z_left)
    t_self = pltpu.make_async_copy(tok_ref, tok_at(l, z), ls.at[1])
    t_self.start()

    def clear(i, _):
        for c in range(2):
            for m in range(2):
                for hh in range(2):
                    wbuf[c, i, m, pl.ds(hh * BLOCK + SENT, BLOCK - SENT), :] = jnp.zeros(
                        (BLOCK - SENT, HALF), BF
                    )
        return 0

    lax.fori_loop(0, 4, clear, 0)

    def piece(yy, hh, m):
        return w_at(k, yy, hh, m)

    def share(at, yy, hh, m):
        return send(piece(yy, hh, m), piece(yy, hh, m), WC + at * 2 + m, core_peer)

    shares = []
    w1ra, w1la, w1rb, w1lb = [], [], [], []

    @pl.when(on_self)
    def _():
        wa_self.wait()

    for m in range(2):

        @pl.when(jnp.logical_not(on_self))
        def _(m=m):
            wa[m].wait_recv()

        w1ra.append(send(piece(y, h, m), piece(y, h, m), W1RA + m, y_right))
        w1la.append(send(piece(y, h, m), piece(y, h, m), W1LA + m, y_left))
        shares.append(share(0, y, h, m))
    t0 = send(tok_ref, tok_at(l, z), T0, x_peer)
    for m in range(2):
        wb[m].wait_recv()
        w1rb.append(send(piece(y, 1 - h, m), piece(y, 1 - h, m), W1RB + m, y_right))
        w1lb.append(send(piece(y, 1 - h, m), piece(y, 1 - h, m), W1LB + m, y_left))
        shares.append(share(1, y, 1 - h, m))

    def spread(i, _):
        raw_copy(i).wait()
        for side in range(2):

            @pl.when(l == side)
            def _(side=side):
                a = raw[i % 2]
                gap = jnp.zeros((CHUNK, BLOCK - SHARD), BF)
                for yy in range(4):
                    parts = []
                    for hh in range(2):
                        start = (2 * (2 * yy + hh) + side) * SHARD
                        parts += [a[:, start : start + SHARD], gap]
                    dl[at_rows(i), pl.ds(yy * PAIR, TILE)] = jnp.concatenate(parts, axis=1)

        @pl.when(i < 2)
        def _():
            raw_copy(i + 2).start()

        return 0

    lax.fori_loop(0, 4, spread, 0)

    t1r.wait_recv()
    t3r = send(tok_half(l, zl, 0), tok_half(l, zl, 0), T3R, z_right)
    t1l.wait_recv()
    t3l = send(tok_half(l, zr, 1), tok_half(l, zr, 1), T3L, z_left)
    w2r, w2l = [], []
    for m in range(2):
        w1ra[m].wait_recv()
        w2r.append(send(piece(yl, h, m), piece(yl, h, m), W2R + m, y_right))
        shares.append(share(2, yl, h, m))
        w1la[m].wait_recv()
        shares.append(share(3, yr, h, m))
    t0.wait_recv()
    t2r = send(tok_at(1 - l, z), tok_at(1 - l, z), T2R, z_right)
    t2l = send(tok_at(1 - l, z), tok_at(1 - l, z), T2L, z_left)
    t3r.wait_recv()
    t3l.wait_recv()
    t5 = send(tok_at(l, zo), tok_at(l, zo), T5, x_peer)
    for m in range(2):
        w1lb[m].wait_recv()
        w2l.append(send(piece(yr, 1 - h, m), piece(yr, 1 - h, m), W2L + m, y_left))
        shares.append(share(4, yr, 1 - h, m))
        w1rb[m].wait_recv()
        shares.append(share(5, yl, 1 - h, m))
    t_self.wait()

    def activate(zz, yy):
        rows = at_rows(zz)
        gu = rows_by_rows(tbuf[0, rows, :], wbuf[0, yy].reshape(PAIR, HALF))
        gu += rows_by_rows(tbuf[1, rows, :], wbuf[1, yy].reshape(PAIR, HALF))
        gate, up = gu[:, :TILE], gu[:, TILE:]
        first = pl.ds(pl.multiple_of(yy * PAIR, TILE), TILE)
        second = pl.ds(pl.multiple_of(yy * PAIR + TILE, TILE), TILE)
        back = dl[rows, first].astype(F32)
        s = jax.nn.sigmoid(gate)
        gs = gate * s
        hid[rows, at_rows(yy)] = (gs * up).astype(BF)
        dl[rows, first] = (back * up * s * (1.0 + gate * (1.0 - s))).astype(BF)
        dl[rows, second] = (back * gs).astype(BF)

    def near_units(zz):
        def step(i, _):
            activate(zz, (y + i + i // 2) % 4)
            return 0

        lax.fori_loop(0, 3, step, 0)

    def hidden_part(zz):
        return hid.at[at_rows(zz), pl.ds(0, COMPACT)]

    def hidden_send(at, zz):
        a = hid[at_rows(zz), :]
        parts = [a[:, q * BLOCK : q * BLOCK + SHARD] for q in range(8)]
        parts.append(jnp.zeros((CHUNK, COMPACT - 8 * SHARD), BF))
        hid[at_rows(zz), pl.ds(0, COMPACT)] = jnp.concatenate(parts, axis=1)
        mine = pltpu.make_async_copy(
            hidden_part(zz), hid_out.at[l, at_rows(zz), :], ls.at[4 + at]
        )
        mine.start()
        return mine, send(hidden_part(zz), hid_out.at[l, at_rows(zz), :], HD + at, x_peer)

    for at in range(12):
        shares[at].wait_recv()
    near_units(z)
    t2r.wait_recv()
    t2l.wait_recv()
    t5.wait_recv()
    near_units(zo)
    for m in range(2):
        w2r[m].wait_recv()
        shares.append(share(6, yo, h, m))
        w2l[m].wait_recv()
        shares.append(share(7, yo, 1 - h, m))
    for at in range(12, 16):
        shares[at].wait_recv()
    activate(zo, yo)
    hidden = [hidden_send(0, zo)]

    def tg_rows(zz, o):
        c = (1 - l) if o == 0 else l
        return jnp.dot(
            dl[at_rows(zz), :], wbuf[c].reshape(2 * HID, HALF), preferred_element_type=F32
        )

    g1 = []
    for o in range(2):
        tgs1[o] = tg_rows(zo, o).astype(BF)
        g1.append((
            send(tgs1.at[o, pl.ds(0, 128), :], tgr1.at[0, o], G1R + o, z_right),
            send(tgs1.at[o, pl.ds(128, 128), :], tgr1.at[1, o], G1L + o, z_left),
        ))

    def far_units(i, _):
        activate((z + i + i // 2) % 4, yo)
        return 0

    lax.fori_loop(0, 3, far_units, 0)
    hidden.append(hidden_send(1, z))

    def gr_group(gi, yy, slot):
        units = pl.ds(pl.multiple_of(yy * PAIR, PAIR), PAIR)
        out = over_rows(dl[:, units], tbuf[1 - k])
        for m in range(2):
            for hh in range(2):
                top = m * TILE + hh * BLOCK
                cs[gi, hh, m] = out[top : top + SENT].astype(BF)
        cp = send(cs.at[gi], cr.at[gi], CC + gi, core_peer)
        out = over_rows(dl[:, units], tbuf[k])
        for m in range(2):
            for hh in range(2):
                top = m * TILE + hh * BLOCK
                own[slot, hh, m] = out[top : top + SENT]
        return cp

    cc = [gr_group(0, yo, 0)]
    near_units(zr)
    hidden.append(hidden_send(2, zr))
    cc[0].wait_recv()
    y1 = []
    for j, (hh, at, to) in enumerate(((1 - h, Y1R, y_right), (h, Y1L, y_left))):
        for m in range(2):
            y1s[j, m] = (own[0, hh, m] + cr[0, hh, m].astype(F32)).astype(BF)
        y1.append(send(y1s.at[j], y1r.at[j], at, to))
    near_units(zl)
    hidden.append(hidden_send(3, zl))

    g2 = []
    for o in range(2):
        for d, (zz, at, to) in enumerate(((zr, G2R, z_right), (zl, G2L, z_left))):
            out = tg_rows(zz, o)
            g1[o][d].wait_recv()
            far = tgr1[d, o].astype(F32)
            lo, hi = out[:128], out[128:]
            if d == 0:
                lo = lo + far
            else:
                hi = hi + far
            tgs2[d, o, pl.ds(0, 128), :] = lo.astype(BF)
            tgs2[d, o, pl.ds(128, 128), :] = hi.astype(BF)
            g2.append(send(tgs2.at[d, o], tgr2.at[d, o], at + o, to))

    y2 = [[], []]
    for d, (yy, at, to) in enumerate(((yr, Y2R, y_right), (yl, Y2L, y_left))):
        slot = 1 - d
        cc.append(gr_group(1 + d, yy, slot))
        cc[1 + d].wait_recv()
        y1[d].wait_recv()
        for j, hh in enumerate((1 - h, h)):
            for m in range(2):
                part = own[slot, hh, m] + cr[1 + d, hh, m].astype(F32)
                if j == d:
                    part = part + y1r[d, m].astype(F32)
                y2s[d, j, m] = part.astype(BF)
            y2[d].append(send(y2s.at[d, j], y2r.at[d, j], at + j, to))

    for o in range(2):
        tgo[o] = tg_rows(z, o)
    cc.append(gr_group(3, y, 1))

    g2[0].wait_recv()
    g2[1].wait_recv()
    txs[...] = (tgo[0] + tgr2[0, 0].astype(F32) + tgr2[1, 0].astype(F32)).astype(BF)
    gx = send(txs, txr, GX, x_peer)
    cc[3].wait_recv()
    xa = remote(xs.at[1], xr.at[1], XA, swap_here)
    xa_self = pltpu.make_async_copy(xs.at[1], xr.at[1], ls.at[8])
    for j, hh in enumerate((1 - h, h)):
        y2[0][j].wait_recv()
        y2[1][j].wait_recv()
        for m in range(2):
            part = own[1, hh, m] + cr[3, hh, m].astype(F32)
            part = part + y2r[0, j, m].astype(F32) + y2r[1, j, m].astype(F32)
            xs[j, m] = part.astype(BF)
        if j == 0:
            xb = send(xs.at[0], xr.at[0], XB, swap_there)

    @pl.when(on_self)
    def _():
        xa_self.start()

    @pl.when(jnp.logical_not(on_self))
    def _():
        xa.start()

    g2[2].wait_recv()
    g2[3].wait_recv()
    gx.wait_recv()
    tg_out[...] = (
        tgo[1] + tgr2[0, 1].astype(F32) + tgr2[1, 1].astype(F32) + txr[...].astype(F32)
    ).astype(BF)
    xb.wait_recv()

    @pl.when(on_self)
    def _():
        xa_self.wait()

    @pl.when(jnp.logical_not(on_self))
    def _():
        xa.wait_recv()

    scale = 1.0 / 128.0
    for m in range(2):
        gr_out[m] = (xr[0, m].astype(F32) + xr[1, m].astype(F32)) * scale

    for mine, cp in hidden:
        mine.wait()
        cp.wait_recv()

    @pl.when(jnp.logical_not(on_self))
    def _():
        for cp in wa + [xa]:
            cp.wait_send()

    for cp in sent:
        cp.wait_send()


def fused(tokens, gate_weight, up_weight, cot):
    vmem = pl.BlockSpec(memory_space=pltpu.VMEM)
    hbm = pl.BlockSpec(memory_space=pl.ANY)
    return pl.pallas_call(
        kernel,
        out_shape=(
            jax.ShapeDtypeStruct((2, TOK, COMPACT), BF),
            jax.ShapeDtypeStruct((CHUNK, HALF), BF),
            jax.ShapeDtypeStruct((2, SENT, HALF), F32),
        ),
        in_specs=[vmem, vmem, vmem, hbm],
        out_specs=(hbm, vmem, vmem),
        scratch_shapes=[
            pltpu.VMEM((2, TOK, HALF), BF),
            pltpu.VMEM((2, 4, 2, TILE, HALF), BF),
            pltpu.VMEM((2, SENT, HALF), BF),
            pltpu.VMEM((TOK, 2 * HID), BF),
            pltpu.VMEM((TOK, HID), BF),
            pltpu.VMEM((2, CHUNK, FF_TILE), BF),
            pltpu.VMEM((2, CHUNK, HALF), BF),
            pltpu.VMEM((2, 2, 128, HALF), BF),
            pltpu.VMEM((2, 2, CHUNK, HALF), BF),
            pltpu.VMEM((2, 2, CHUNK, HALF), BF),
            pltpu.VMEM((2, CHUNK, HALF), F32),
            pltpu.VMEM((CHUNK, HALF), BF),
            pltpu.VMEM((CHUNK, HALF), BF),
            pltpu.VMEM((4, 2, 2, SENT, HALF), BF),
            pltpu.VMEM((4, 2, 2, SENT, HALF), BF),
            pltpu.VMEM((2, 2, 2, SENT, HALF), F32),
            pltpu.VMEM((2, 2, SENT, HALF), BF),
            pltpu.VMEM((2, 2, SENT, HALF), BF),
            pltpu.VMEM((2, 2, 2, SENT, HALF), BF),
            pltpu.VMEM((2, 2, 2, SENT, HALF), BF),
            pltpu.VMEM((2, 2, SENT, HALF), BF),
            pltpu.VMEM((2, 2, SENT, HALF), BF),
            pltpu.SemaphoreType.DMA((N_SEM,)),
            pltpu.SemaphoreType.DMA((N_SEM,)),
            pltpu.SemaphoreType.DMA((9,)),
        ],
        compiler_params=pltpu.CompilerParams(
            collective_id=0, has_side_effects=True, vmem_limit_bytes=64 * 1024 * 1024,
        ),
        cost_estimate=pl.CostEstimate(
            flops=12 * TOK * HID * 2 * HALF, bytes_accessed=12 * 1024 * 1024,
            transcendentals=TOK * HID,
        ),
        name="swiglu_grid",
    )(tokens, gate_weight, up_weight, cot)


def merge_kernel(hid_ref, out_ref):
    first, second = hid_ref[0], hid_ref[1]
    parts = []
    for q in range(8):
        cols = slice(q * SHARD, (q + 1) * SHARD)
        parts += [first[:, cols], second[:, cols]]
    out_ref[...] = jnp.concatenate(parts, axis=1)


def merge(hid):
    rows = 256
    return pl.pallas_call(
        merge_kernel,
        out_shape=jax.ShapeDtypeStruct((TOK, FF_TILE), BF),
        grid=(TOK // rows,),
        in_specs=[pl.BlockSpec((2, rows, COMPACT), lambda i: (0, i, 0))],
        out_specs=pl.BlockSpec((rows, FF_TILE), lambda i: (i, 0)),
        name="merge_hidden",
    )(hid)


def per_device(tokens, gate_weight, up_weight, cotangent):
    hid, token_grad, grads = fused(tokens, gate_weight, up_weight, cotangent)
    return merge(hid), token_grad, grads[0, :SHARD], grads[1, :SHARD]


def solution(mesh):
    in_specs = (
        P(("dp", "trow"), "tcol"),
        P(("trow", "dp"), "tcol"),
        P(("trow", "dp"), "tcol"),
        P("dp", "trow"),
    )
    out_specs = (
        P("dp", "trow"),
        P(("dp", "trow"), "tcol"),
        P(("trow", "dp"), "tcol"),
        P(("trow", "dp"), "tcol"),
    )
    return jax.shard_map(
        per_device, mesh=mesh, in_specs=in_specs, out_specs=out_specs, check_vma=False
    )
```

time: 772 us -> 151 us (0.20)
  the two profiles are of different devices: /device:TPU:0 before, /device:TPU:1 now
where the time goes in v2:
time: 151 us
  Pallas kernels  136 us (90%)
  local copies, waits for them, and re-layouts  13.8 us (9%)
    pallas_call x1, Pallas kernels, fused(): pl.pallas_call(kernel, out_shape=(jax.ShapeDtypeStruct((2, TOK, COMPACT),...  131 us
    unnamed x7, local copies, waits for them, and re-layouts  12.7 us
    pallas_call x1, Pallas kernels, merge(): pl.pallas_call(merge_kernel, out_shape=jax.ShapeDtypeStruct((TOK, FF_TILE...  5.41 us

profile of v2, /device:TPU:1, one launch (start us, length us, event | category | flops | bytes accessed | tf_op | source)
XLA Modules:
  0.0 150.8 jit_solution(4222240031890091923)
XLA Ops:
  0.6 5.8 %copy.8.cot_ref = bf16[1024,1728]{1,0:T(8,128)(2,1)} copy(bf16[1024,1728]{0,1:T(8,128)(2,1)} %param.7) | data formatting | bytes 7077888 | tf_op args[3]
  6.4 131.0 %swiglu_grid.1 = (bf16[2,1024,896]{2,1,0:T(8,128)(2,1)}, bf16[256,1280]{1,0:T(8,128)(2,1)}, f32[2,112,1280]{2,1,0:T(8,128)}) custom-call(bf16[256,1280]{1,0:T(8,128)(2,1)} %tok_ref.1, bf16[108,1280]{1,0:T(8,128)(2,1)} %gw_ref.1, bf16[108,1280]{1,0:T(8,128)(2,1)} %uw_ref.1, bf16[1024,1728]{1,0:T(8,128)(2,1)} %copy.8.cot_ref), custom_call_target="tpu_custom_call" | custom-call | flops 32212254720 | bytes 12582912 | tf_op jit(solution)/shard_map/swiglu_grid/pallas_call | solution.py:443
  137.4 5.4 %merge_hidden.1 = bf16[1024,1728]{1,0:T(8,128)(2,1)} custom-call(bf16[2,1024,896]{2,1,0:T(8,128)(2,1)} %get-tuple-element.7.hid_ref), custom_call_target="tpu_custom_call" | custom-call | tf_op jit(solution)/shard_map/merge_hidden/pallas_call | solution.py:501
  142.8 0.0 copy-start
  142.8 0.0 copy-start.1
  142.8 6.0 %copy.9 = bf16[1024,1728]{0,1:T(8,128)(2,1)} copy(bf16[1024,1728]{1,0:T(8,128)(2,1)} %merge_hidden.1) | data formatting | bytes 7077888
  148.9 0.0 copy-done
  148.9 1.1 slice_bitcast_fusion
  149.9 0.0 copy-done.1
  149.9 0.8 copy.11
Async XLA Ops:
  142.8 6.0 %copy-start = (f32[2,112,1280]{2,1,0:T(8,128)S(1)}, f32[2,112,1280]{2,1,0:T(8,128)}, u32[]{:S(2)}) copy-start(f32[2,112,1280]{2,1,0:T(8,128)} %get-tuple-element.9) | copy-start | bytes 3440644
  142.8 7.1 %copy-start.1 = (bf16[256,1280]{1,0:T(8,128)(2,1)S(1)}, bf16[256,1280]{1,0:T(8,128)(2,1)}, u32[]{:S(2)}) copy-start(bf16[256,1280]{1,0:T(8,128)(2,1)} %get-tuple-element.21) | copy-start | bytes 1966084

commit v3 on v2

v3 whole, which is shorter than its diff:
```python
import jax
import jax.numpy as jnp
from jax import lax
from jax.experimental import pallas as pl
from jax.experimental.pallas import tpu as pltpu
from jax.sharding import PartitionSpec as P

BF = jnp.bfloat16
F32 = jnp.float32
MESH = pl.DeviceIdType.MESH

SHARD = 108
SENT = 112
BLOCK = 128
HALF = 1280
CHUNK = 256
TOK = 1024
TILE = 256
HID = 1024
FF_TILE = 16 * SHARD

counts = []


def place(count=1):
    counts.append(count)
    return sum(counts) - count


T0, T1R, T1L, T2R, T2L, T3R, T3L, T5 = [place() for _ in range(8)]
WA, WB = place(2), place(2)
W1RA, W1LA, W1RB, W1LB = [place(2) for _ in range(4)]
W2RA, W2LA, W2RB, W2LB = [place() for _ in range(4)]
WC = place(16)
HD = place(8)
G1R, G1L, G2R, G2L = [place(2) for _ in range(4)]
GX = place()
CC = place(4)
Y1R, Y1L = place(), place()
Y2R, Y2L = place(2), place(2)
XA, XB = place(), place()
N_SEM = sum(counts)


def rows_by_rows(left, right):
    return lax.dot_general(
        left, right, (((1,), (1,)), ((), ())), preferred_element_type=F32
    )


def over_rows(left, right):
    return lax.dot_general(
        left, right, (((0,), (0,)), ((), ())), preferred_element_type=F32
    )


def at_rows(i, n=CHUNK):
    return pl.ds(pl.multiple_of(i * n, n), n)


def kernel(
    tok_ref, gw_ref, uw_ref, cot_ref,
    hid_out, tg_out, gr_out,
    tbuf, wbuf, wsrc, dl, hid, raw,
    tgs1, tgr1, tgs2, tgr2, tgo, txs, txr,
    cs, cr, own, y1s, y1r, y2s, y2r, xs, xr,
    ss, rs, ls,
):
    dp = lax.axis_index("dp")
    z = lax.axis_index("trow")
    l = lax.axis_index("tcol")
    k = dp % 2
    h = (dp // 2) % 2
    y = dp // 4

    def dev(y_, h_, k_, z_, l_):
        return {"dp": (y_ * 2 + h_) * 2 + k_, "trow": z_, "tcol": l_}

    zr, zl, zo = (z + 1) % 4, (z + 3) % 4, (z + 2) % 4
    yr, yl, yo = (y + 1) % 4, (y + 3) % 4, (y + 2) % 4
    z_right, z_left = dev(y, h, k, zr, l), dev(y, h, k, zl, l)
    y_right, y_left = dev(yr, h, k, z, l), dev(yl, h, k, z, l)
    core_peer = dev(y, h, 1 - k, z, l)
    x_peer = dev(y, h, k, z, 1 - l)
    swap_here = dev(y, h, l, z, k)
    swap_there = dev(y, 1 - h, l, z, k)
    on_self = k == l
    sent = []

    def remote(src, dst, at, to):
        return pltpu.make_async_remote_copy(
            src_ref=src, dst_ref=dst, send_sem=ss.at[at], recv_sem=rs.at[at],
            device_id=to, device_id_type=MESH,
        )

    def send(src, dst, at, to):
        cp = remote(src, dst, at, to)
        cp.start()
        sent.append(cp)
        return cp

    barrier = pltpu.get_barrier_semaphore()
    for peer in (z_right, z_left, y_right, y_left, core_peer, x_peer, swap_there):
        pl.semaphore_signal(barrier, inc=1, device_id=peer, device_id_type=MESH)

    @pl.when(jnp.logical_not(on_self))
    def _():
        pl.semaphore_signal(barrier, inc=1, device_id=swap_here, device_id_type=MESH)

    def raw_copy(i):
        slot = i % 2
        return pltpu.make_async_copy(
            cot_ref.at[at_rows(i, 4 * SHARD), :], raw.at[slot], ls.at[2 + slot]
        )

    raw_copy(0).start()
    raw_copy(1).start()
    for m, ref in enumerate((gw_ref, uw_ref)):
        wsrc[m, pl.ds(96, 16), :] = jnp.zeros((16, HALF), BF)
        wsrc[m, pl.ds(0, SHARD), :] = ref[...]

    @pl.when(on_self)
    def _():
        pl.semaphore_wait(barrier, 7)

    @pl.when(jnp.logical_not(on_self))
    def _():
        pl.semaphore_wait(barrier, 8)

    def tok_at(c, zz):
        return tbuf.at[c, at_rows(zz), :]

    def tok_half(c, zz, part):
        return tbuf.at[c, pl.ds(pl.multiple_of(zz * CHUNK + part * 128, 128), 128), :]

    def w_at(c, yy, hh, m):
        return wbuf.at[c, yy, hh, m, pl.ds(0, SENT), :]

    wa = [remote(wsrc.at[m], w_at(l, y, h, m), WA + m, swap_here) for m in range(2)]
    wa_self = pltpu.make_async_copy(
        wsrc, wbuf.at[l, y, h, :, pl.ds(0, SENT), :], ls.at[0]
    )

    @pl.when(on_self)
    def _():
        wa_self.start()

    @pl.when(jnp.logical_not(on_self))
    def _():
        wa[0].start()
        wa[1].start()

    t1r = send(tok_ref, tok_at(l, z), T1R, z_right)
    t1l = send(tok_ref, tok_at(l, z), T1L, z_left)
    t_self = pltpu.make_async_copy(tok_ref, tok_at(l, z), ls.at[1])
    t_self.start()

    def clear(i, _):
        for c in range(2):
            for hh in range(2):
                for m in range(2):
                    wbuf[c, i, hh, m, pl.ds(SENT, BLOCK - SENT), :] = jnp.zeros(
                        (BLOCK - SENT, HALF), BF
                    )
        return 0

    lax.fori_loop(0, 4, clear, 0)

    def piece(yy, hh, m):
        return w_at(k, yy, hh, m)

    def pass_on(yy, hh, m, at, to):
        return send(piece(yy, hh, m), piece(yy, hh, m), at, to)

    def share(at, yy, hh, m):
        return pass_on(yy, hh, m, WC + at * 2 + m, core_peer)

    @pl.when(on_self)
    def _():
        wa_self.wait()

    own_a, own_b, near_a, near_b = [], [], [], []
    w1ra, w1la, w1rb, w1lb = [], [], [], []
    for m in range(2):

        @pl.when(jnp.logical_not(on_self))
        def _(m=m):
            wa[m].wait_recv()

        w1ra.append(pass_on(y, h, m, W1RA + m, y_right))
        w1la.append(pass_on(y, h, m, W1LA + m, y_left))
        own_a.append(share(0, y, h, m))
    t0 = send(tok_ref, tok_at(l, z), T0, x_peer)

    def spread(i, _):
        raw_copy(i).wait()
        for side in range(2):

            @pl.when(l == side)
            def _(side=side):
                a = raw[i % 2]
                gap = jnp.zeros((BLOCK - SHARD, TOK), BF)
                for hh in range(2):
                    start = (2 * hh + side) * SHARD
                    dl[i, hh, 0] = jnp.concatenate([a[start : start + SHARD], gap], axis=0)

        @pl.when(i < 2)
        def _():
            raw_copy(i + 2).start()

        return 0

    lax.fori_loop(0, 4, spread, 0)

    t1r.wait_recv()
    t3r = send(tok_half(l, zl, 0), tok_half(l, zl, 0), T3R, z_right)
    t1l.wait_recv()
    t3l = send(tok_half(l, zr, 1), tok_half(l, zr, 1), T3L, z_left)
    for m in range(2):
        w1ra[m].wait_recv()
        if m == 0:
            w2ra = pass_on(yl, h, 0, W2RA, y_right)
        near_a.append(share(2, yl, h, m))
        w1la[m].wait_recv()
        if m == 1:
            w2la = pass_on(yr, h, 1, W2LA, y_left)
        near_a.append(share(3, yr, h, m))
    t0.wait_recv()
    t2r = send(tok_at(1 - l, z), tok_at(1 - l, z), T2R, z_right)
    t2l = send(tok_at(1 - l, z), tok_at(1 - l, z), T2L, z_left)
    wb = [send(wsrc.at[m], w_at(l, y, h, m), WB + m, swap_there) for m in range(2)]
    t3r.wait_recv()
    t3l.wait_recv()
    t5 = send(tok_at(l, zo), tok_at(l, zo), T5, x_peer)
    for m in range(2):
        wb[m].wait_recv()
        w1rb.append(pass_on(y, 1 - h, m, W1RB + m, y_right))
        w1lb.append(pass_on(y, 1 - h, m, W1LB + m, y_left))
        own_b.append(share(1, y, 1 - h, m))
    w2ra.wait_recv()
    far_a = [share(6, yo, h, 0)]
    w2la.wait_recv()
    far_a.append(share(6, yo, h, 1))
    t_self.wait()

    def activate(zz, yy, hh):
        cols = at_rows(zz)
        gu = rows_by_rows(wbuf[0, yy, hh].reshape(TILE, HALF), tbuf[0, cols, :])
        gu += rows_by_rows(wbuf[1, yy, hh].reshape(TILE, HALF), tbuf[1, cols, :])
        gate, up = gu[:BLOCK], gu[BLOCK:]
        back = dl[yy, hh, 0, :, cols].astype(F32)
        s = jax.nn.sigmoid(gate)
        gs = gate * s
        hid[hh, yy, :, cols] = (gs * up).astype(BF)
        dl[yy, hh, 0, :, cols] = (back * up * s * (1.0 + gate * (1.0 - s))).astype(BF)
        dl[yy, hh, 1, :, cols] = (back * gs).astype(BF)

    def blocks(zz, hh, count):
        def step(i, _):
            activate(zz, (y + i + i // 2 - 2 * (i // 3)) % 4, hh)
            return 0

        lax.fori_loop(0, count, step, 0)

    def hidden_send(at, zz, hh):
        part = hid.at[hh, :, pl.ds(0, SENT), at_rows(zz)]
        there = hid_out.at[l, hh, :, :, at_rows(zz)]
        mine = pltpu.make_async_copy(part, there, ls.at[4 + at])
        mine.start()
        return mine, send(part, there, HD + at, x_peer)

    def arrived(copies):
        for cp in copies:
            cp.wait_recv()

    arrived(own_a + near_a + far_a)
    blocks(z, h, 4)
    t2r.wait_recv()
    blocks(zl, h, 4)
    for m in range(2):
        w1rb[m].wait_recv()
        if m == 0:
            w2rb = pass_on(yl, 1 - h, 0, W2RB, y_right)
        near_b.append(share(4, yl, 1 - h, m))
        w1lb[m].wait_recv()
        if m == 1:
            w2lb = pass_on(yr, 1 - h, 1, W2LB, y_left)
        near_b.append(share(5, yr, 1 - h, m))
    t2l.wait_recv()
    blocks(zr, h, 4)
    t5.wait_recv()
    hidden = [hidden_send(0, z, h), hidden_send(1, zl, h), hidden_send(2, zr, h)]
    blocks(zo, h, 4)
    hidden.append(hidden_send(3, zo, h))
    arrived(own_b + near_b)
    blocks(zo, 1 - h, 3)
    w2rb.wait_recv()
    far_b = [share(7, yo, 1 - h, 0)]
    w2lb.wait_recv()
    far_b.append(share(7, yo, 1 - h, 1))
    arrived(far_b)
    activate(zo, yo, 1 - h)
    hidden.append(hidden_send(4, zo, 1 - h))

    def tg_rows(zz, o):
        c = (1 - l) if o == 0 else l
        return over_rows(
            dl[:, :, :, :, at_rows(zz)].reshape(2 * HID, CHUNK), wbuf[c].reshape(2 * HID, HALF)
        )

    g1 = []
    for o in range(2):
        tgs1[o] = tg_rows(zo, o).astype(BF)
        g1.append((
            send(tgs1.at[o, pl.ds(0, 128), :], tgr1.at[0, o], G1R + o, z_right),
            send(tgs1.at[o, pl.ds(128, 128), :], tgr1.at[1, o], G1L + o, z_left),
        ))

    def far_units(i, _):
        activate((z + i + i // 2) % 4, yo, 1 - h)
        return 0

    lax.fori_loop(0, 3, far_units, 0)

    def gr_half(yy, c):
        return jnp.dot(dl[yy].reshape(2 * TILE, TOK), tbuf[c], preferred_element_type=F32)

    def gr_other(gi, yy):
        out = gr_half(yy, 1 - k)
        for hh in range(2):
            for m in range(2):
                top = hh * TILE + m * BLOCK
                cs[gi, hh, m] = out[top : top + SENT].astype(BF)
        return send(cs.at[gi], cr.at[gi], CC + gi, core_peer)

    def gr_own(slot, yy):
        out = gr_half(yy, k)
        for hh in range(2):
            for m in range(2):
                top = hh * TILE + m * BLOCK
                own[slot, hh, m] = out[top : top + SENT]

    of_j = (1 - h, h)
    cc = [gr_other(0, yo)]
    gr_own(0, yo)
    cc[0].wait_recv()
    y1 = []
    for m, (at, to) in enumerate(((Y1R, y_right), (Y1L, y_left))):
        for j, hh in enumerate(of_j):
            y1s[m, j] = (own[0, hh, m] + cr[0, hh, m].astype(F32)).astype(BF)
        y1.append(send(y1s.at[m], y1r.at[m], at, to))

    for at, zz in ((5, z), (6, zr), (7, zl)):
        blocks(zz, 1 - h, 3)
        hidden.append(hidden_send(at, zz, 1 - h))
    cc.append(gr_other(1, yr))
    cc.append(gr_other(2, yl))

    g2 = []

    def tg_near(o):
        for d, (zz, at, to) in enumerate(((zr, G2R, z_right), (zl, G2L, z_left))):
            out = tg_rows(zz, o)
            g1[o][d].wait_recv()
            far = tgr1[d, o].astype(F32)
            lo, hi = out[:128], out[128:]
            if d == 0:
                lo = lo + far
            else:
                hi = hi + far
            tgs2[d, o, pl.ds(0, 128), :] = lo.astype(BF)
            tgs2[d, o, pl.ds(128, 128), :] = hi.astype(BF)
            g2.append(send(tgs2.at[d, o], tgr2.at[d, o], at + o, to))

    tg_near(0)
    gr_own(1, yr)
    gr_own(0, yl)
    y2 = []
    for j, hh in enumerate(of_j):
        for d, (at, to) in enumerate(((Y2R, y_right), (Y2L, y_left))):
            if j == 0:
                cc[1 + d].wait_recv()
                y1[d].wait_recv()
            for m in range(2):
                part = own[1 - d, hh, m] + cr[1 + d, hh, m].astype(F32)
                if m == d:
                    part = part + y1r[d, j].astype(F32)
                y2s[d, j, m] = part.astype(BF)
            y2.append(send(y2s.at[d, j], y2r.at[d, j], at + j, to))

    tg_near(1)
    cc.append(gr_other(3, y))
    for o in range(2):
        tgo[o] = tg_rows(z, o)
    gr_own(1, y)

    g2[0].wait_recv()
    g2[1].wait_recv()
    txs[...] = (tgo[0] + tgr2[0, 0].astype(F32) + tgr2[1, 0].astype(F32)).astype(BF)
    gx = send(txs, txr, GX, x_peer)
    cc[3].wait_recv()
    xa = remote(xs.at[1], xr.at[1], XA, swap_here)
    xa_self = pltpu.make_async_copy(xs.at[1], xr.at[1], ls.at[12])
    for j, hh in enumerate(of_j):
        y2[2 * j].wait_recv()
        y2[2 * j + 1].wait_recv()
        for m in range(2):
            part = own[1, hh, m] + cr[3, hh, m].astype(F32)
            part = part + y2r[0, j, m].astype(F32) + y2r[1, j, m].astype(F32)
            xs[j, m] = part.astype(BF)
        if j == 0:
            xb = send(xs.at[0], xr.at[0], XB, swap_there)

    @pl.when(on_self)
    def _():
        xa_self.start()

    @pl.when(jnp.logical_not(on_self))
    def _():
        xa.start()

    g2[2].wait_recv()
    g2[3].wait_recv()
    gx.wait_recv()
    tg_out[...] = (
        tgo[1] + tgr2[0, 1].astype(F32) + tgr2[1, 1].astype(F32) + txr[...].astype(F32)
    ).astype(BF)
    xb.wait_recv()

    @pl.when(on_self)
    def _():
        xa_self.wait()

    @pl.when(jnp.logical_not(on_self))
    def _():
        xa.wait_recv()

    scale = 1.0 / 128.0
    for m in range(2):
        gr_out[m] = (xr[0, m].astype(F32) + xr[1, m].astype(F32)) * scale

    for mine, cp in hidden:
        mine.wait()
        cp.wait_recv()

    @pl.when(jnp.logical_not(on_self))
    def _():
        for cp in wa + [xa]:
            cp.wait_send()

    for cp in sent:
        cp.wait_send()


def fused(tokens, gate_weight, up_weight, cot):
    vmem = pl.BlockSpec(memory_space=pltpu.VMEM)
    hbm = pl.BlockSpec(memory_space=pl.ANY)
    return pl.pallas_call(
        kernel,
        out_shape=(
            jax.ShapeDtypeStruct((2, 2, 4, SENT, TOK), BF),
            jax.ShapeDtypeStruct((CHUNK, HALF), BF),
            jax.ShapeDtypeStruct((2, SENT, HALF), F32),
        ),
        in_specs=[vmem, vmem, vmem, hbm],
        out_specs=(hbm, vmem, vmem),
        scratch_shapes=[
            pltpu.VMEM((2, TOK, HALF), BF),
            pltpu.VMEM((2, 4, 2, 2, BLOCK, HALF), BF),
            pltpu.VMEM((2, SENT, HALF), BF),
            pltpu.VMEM((4, 2, 2, BLOCK, TOK), BF),
            pltpu.VMEM((2, 4, BLOCK, TOK), BF),
            pltpu.VMEM((2, 4 * SHARD, TOK), BF),
            pltpu.VMEM((2, CHUNK, HALF), BF),
            pltpu.VMEM((2, 2, 128, HALF), BF),
            pltpu.VMEM((2, 2, CHUNK, HALF), BF),
            pltpu.VMEM((2, 2, CHUNK, HALF), BF),
            pltpu.VMEM((2, CHUNK, HALF), F32),
            pltpu.VMEM((CHUNK, HALF), BF),
            pltpu.VMEM((CHUNK, HALF), BF),
            pltpu.VMEM((4, 2, 2, SENT, HALF), BF),
            pltpu.VMEM((4, 2, 2, SENT, HALF), BF),
            pltpu.VMEM((2, 2, 2, SENT, HALF), F32),
            pltpu.VMEM((2, 2, SENT, HALF), BF),
            pltpu.VMEM((2, 2, SENT, HALF), BF),
            pltpu.VMEM((2, 2, 2, SENT, HALF), BF),
            pltpu.VMEM((2, 2, 2, SENT, HALF), BF),
            pltpu.VMEM((2, 2, SENT, HALF), BF),
            pltpu.VMEM((2, 2, SENT, HALF), BF),
            pltpu.SemaphoreType.DMA((N_SEM,)),
            pltpu.SemaphoreType.DMA((N_SEM,)),
            pltpu.SemaphoreType.DMA((13,)),
        ],
        compiler_params=pltpu.CompilerParams(
            collective_id=0, has_side_effects=True, vmem_limit_bytes=64 * 1024 * 1024,
        ),
        cost_estimate=pl.CostEstimate(
            flops=12 * TOK * HID * 2 * HALF, bytes_accessed=12 * 1024 * 1024,
            transcendentals=TOK * HID,
        ),
        name="swiglu_grid",
    )(tokens, gate_weight, up_weight, cot)


def merge_kernel(hid_ref, out_ref):
    parts = [hid_ref[side, hh, 0, :SHARD] for hh in range(2) for side in range(2)]
    out_ref[...] = jnp.concatenate(parts, axis=0)


def merge(hid):
    return pl.pallas_call(
        merge_kernel,
        out_shape=jax.ShapeDtypeStruct((FF_TILE, TOK), BF),
        grid=(4,),
        in_specs=[pl.BlockSpec((2, 2, 1, SENT, TOK), lambda i: (0, 0, i, 0, 0))],
        out_specs=pl.BlockSpec((4 * SHARD, TOK), lambda i: (i, 0)),
        name="merge_hidden",
    )(hid)


def per_device(tokens, gate_weight, up_weight, cotangent):
    hid, token_grad, grads = fused(tokens, gate_weight, up_weight, cotangent.T)
    return merge(hid).T, token_grad, grads[0, :SHARD], grads[1, :SHARD]


def solution(mesh):
    in_specs = (
        P(("dp", "trow"), "tcol"),
        P(("trow", "dp"), "tcol"),
        P(("trow", "dp"), "tcol"),
        P("dp", "trow"),
    )
    out_specs = (
        P("dp", "trow"),
        P(("dp", "trow"), "tcol"),
        P(("trow", "dp"), "tcol"),
        P(("trow", "dp"), "tcol"),
    )
    return jax.shard_map(
        per_device, mesh=mesh, in_specs=in_specs, out_specs=out_specs, check_vma=False
    )
```

time: 151 us -> 138 us (0.914)
  the two profiles are of different devices: /device:TPU:1 before, /device:TPU:0 now
where the time goes in v3:
time: 138 us; the launch traced here: 137 us
  Pallas kernels  134 us (97%)
  local copies, waits for them, and re-layouts  1.92 us (1%)
    pallas_call x1, Pallas kernels, fused(): pl.pallas_call(kernel, out_shape=(jax.ShapeDtypeStruct((2, 2, 4, SENT, TO...  130 us
    pallas_call x1, Pallas kernels, merge(): pl.pallas_call(merge_kernel, out_shape=jax.ShapeDtypeStruct((FF_TILE, TOK...  4.57 us

profile of v3, /device:TPU:0, one launch (start us, length us, event | category | flops | bytes accessed | tf_op | source)
XLA Modules:
  0.0 136.9 jit_solution(146830719517413384)
XLA Ops:
  0.6 129.7 %swiglu_grid.1 = (bf16[2,2,4,112,1024]{4,3,2,1,0:T(8,128)(2,1)}, bf16[256,1280]{1,0:T(8,128)(2,1)}, f32[2,112,1280]{2,1,0:T(8,128)}) custom-call(bf16[256,1280]{1,0:T(8,128)(2,1)} %tok_ref.1, bf16[108,1280]{1,0:T(8,128)(2,1)} %gw_ref.1, bf16[108,1280]{1,0:T(8,128)(2,1)} %uw_ref.1, bf16[1728,1024]{1,0:T(8,128)(2,1)} %bitcast.7), custom_call_target="tpu_custom_call" | custom-call | flops 32212254720 | bytes 12582912 | tf_op jit(solution)/shard_map/swiglu_grid/pallas_call | solution.py:458
  130.4 0.0 copy-start
  130.4 0.0 copy-start.1
  130.4 4.6 %merge_hidden.1 = bf16[1728,1024]{1,0:T(8,128)(2,1)} custom-call(bf16[2,2,4,112,1024]{4,3,2,1,0:T(8,128)(2,1)} %get-tuple-element.7.hid_ref), custom_call_target="tpu_custom_call" | custom-call | tf_op jit(solution)/shard_map/merge_hidden/pallas_call | solution.py:511
  135.0 0.0 copy-done
  135.0 1.1 slice_bitcast_fusion
  136.0 0.0 copy-done.1
  136.0 0.8 copy.9
Async XLA Ops:
  130.4 4.6 %copy-start = (f32[2,112,1280]{2,1,0:T(8,128)S(1)}, f32[2,112,1280]{2,1,0:T(8,128)}, u32[]{:S(2)}) copy-start(f32[2,112,1280]{2,1,0:T(8,128)} %get-tuple-element.9) | copy-start | bytes 3440644
  130.4 5.7 %copy-start.1 = (bf16[256,1280]{1,0:T(8,128)(2,1)S(1)}, bf16[256,1280]{1,0:T(8,128)(2,1)}, u32[]{:S(2)}) copy-start(bf16[256,1280]{1,0:T(8,128)(2,1)} %get-tuple-element.17) | copy-start | bytes 1966084

commit v4 on v3

--- a/solution.py
+++ b/solution.py
@@ -10,13 +10,12 @@
 MESH = pl.DeviceIdType.MESH
 
 SHARD = 108
-SENT = 112
-BLOCK = 128
+BLOCK = 112
 HALF = 1280
 CHUNK = 256
 TOK = 1024
-TILE = 256
-HID = 1024
+TILE = 2 * BLOCK
+HID = 8 * BLOCK
 FF_TILE = 16 * SHARD
 
 counts = []
@@ -27,7 +26,7 @@
     return sum(counts) - count
 
 
-T0, T1R, T1L, T2R, T2L, T3R, T3L, T5 = [place() for _ in range(8)]
+T0, T1R, T1L, T2R, T2L, T3R, T3L, T4R, T4L = [place() for _ in range(9)]
 WA, WB = place(2), place(2)
 W1RA, W1LA, W1RB, W1LB = [place(2) for _ in range(4)]
 W2RA, W2LA, W2RB, W2LB = [place() for _ in range(4)]
@@ -37,8 +36,8 @@
 GX = place()
 CC = place(4)
 Y1R, Y1L = place(), place()
-Y2R, Y2L = place(2), place(2)
-XA, XB = place(), place()
+Y2R, Y2L = place(4), place(4)
+XA, XB = place(2), place(2)
 N_SEM = sum(counts)
 
 
@@ -134,12 +133,15 @@
         return tbuf.at[c, pl.ds(pl.multiple_of(zz * CHUNK + part * 128, 128), 128), :]
 
     def w_at(c, yy, hh, m):
-        return wbuf.at[c, yy, hh, m, pl.ds(0, SENT), :]
+        return wbuf.at[c, yy, hh, m]
 
     wa = [remote(wsrc.at[m], w_at(l, y, h, m), WA + m, swap_here) for m in range(2)]
     wa_self = pltpu.make_async_copy(
-        wsrc, wbuf.at[l, y, h, :, pl.ds(0, SENT), :], ls.at[0]
+        wsrc, wbuf.at[l, y, h], ls.at[0]
     )
+
+    wb = [remote(wsrc.at[m], w_at(l, y, h, m), WB + m, swap_there) for m in range(2)]
+    sent.extend(wb)
 
     @pl.when(on_self)
     def _():
@@ -149,23 +151,17 @@
     def _():
         wa[0].start()
         wa[1].start()
+        wb[0].start()
+        wb[1].start()
+
+    t0 = remote(tok_ref, tok_at(l, z), T0, x_peer)
+    sent.append(t0)
 
     t1r = send(tok_ref, tok_at(l, z), T1R, z_right)
     t1l = send(tok_ref, tok_at(l, z), T1L, z_left)
     t_self = pltpu.make_async_copy(tok_ref, tok_at(l, z), ls.at[1])
     t_self.start()
 
-    def clear(i, _):
-        for c in range(2):
-            for hh in range(2):
-                for m in range(2):
-                    wbuf[c, i, hh, m, pl.ds(SENT, BLOCK - SENT), :] = jnp.zeros(
-                        (BLOCK - SENT, HALF), BF
-                    )
-        return 0
-
-    lax.fori_loop(0, 4, clear, 0)
-
     def piece(yy, hh, m):
         return w_at(k, yy, hh, m)
 
@@ -190,7 +186,7 @@
         w1ra.append(pass_on(y, h, m, W1RA + m, y_right))
         w1la.append(pass_on(y, h, m, W1LA + m, y_left))
         own_a.append(share(0, y, h, m))
-    t0 = send(tok_ref, tok_at(l, z), T0, x_peer)
+    t0.start()
 
     def spread(i, _):
         raw_copy(i).wait()
@@ -228,10 +224,14 @@
     t0.wait_recv()
     t2r = send(tok_at(1 - l, z), tok_at(1 - l, z), T2R, z_right)
     t2l = send(tok_at(1 - l, z), tok_at(1 - l, z), T2L, z_left)
-    wb = [send(wsrc.at[m], w_at(l, y, h, m), WB + m, swap_there) for m in range(2)]
+
+    @pl.when(on_self)
+    def _():
+        wb[0].start()
+        wb[1].start()
+
     t3r.wait_recv()
     t3l.wait_recv()
-    t5 = send(tok_at(l, zo), tok_at(l, zo), T5, x_peer)
     for m in range(2):
         wb[m].wait_recv()
         w1rb.append(pass_on(y, 1 - h, m, W1RB + m, y_right))
@@ -263,7 +263,7 @@
         lax.fori_loop(0, count, step, 0)
 
     def hidden_send(at, zz, hh):
-        part = hid.at[hh, :, pl.ds(0, SENT), at_rows(zz)]
+        part = hid.at[hh, :, :, at_rows(zz)]
         there = hid_out.at[l, hh, :, :, at_rows(zz)]
         mine = pltpu.make_async_copy(part, there, ls.at[4 + at])
         mine.start()
@@ -275,8 +275,13 @@
 
     arrived(own_a + near_a + far_a)
     blocks(z, h, 4)
+    hidden = [hidden_send(0, z, h)]
     t2r.wait_recv()
+    t4r = send(tok_half(1 - l, zl, 0), tok_half(1 - l, zl, 0), T4R, z_right)
+    t2l.wait_recv()
+    t4l = send(tok_half(1 - l, zr, 1), tok_half(1 - l, zr, 1), T4L, z_left)
     blocks(zl, h, 4)
+    hidden.append(hidden_send(1, zl, h))
     for m in range(2):
         w1rb[m].wait_recv()
         if m == 0:
@@ -286,10 +291,10 @@
         if m == 1:
             w2lb = pass_on(yr, 1 - h, 1, W2LB, y_left)
         near_b.append(share(5, yr, 1 - h, m))
-    t2l.wait_recv()
     blocks(zr, h, 4)
-    t5.wait_recv()
-    hidden = [hidden_send(0, z, h), hidden_send(1, zl, h), hidden_send(2, zr, h)]
+    hidden.append(hidden_send(2, zr, h))
+    t4r.wait_recv()
+    t4l.wait_recv()
     blocks(zo, h, 4)
     hidden.append(hidden_send(3, zo, h))
     arrived(own_b + near_b)
@@ -308,20 +313,6 @@
             dl[:, :, :, :, at_rows(zz)].reshape(2 * HID, CHUNK), wbuf[c].reshape(2 * HID, HALF)
         )
 
-    g1 = []
-    for o in range(2):
-        tgs1[o] = tg_rows(zo, o).astype(BF)
-        g1.append((
-            send(tgs1.at[o, pl.ds(0, 128), :], tgr1.at[0, o], G1R + o, z_right),
-            send(tgs1.at[o, pl.ds(128, 128), :], tgr1.at[1, o], G1L + o, z_left),
-        ))
-
-    def far_units(i, _):
-        activate((z + i + i // 2) % 4, yo, 1 - h)
-        return 0
-
-    lax.fori_loop(0, 3, far_units, 0)
-
     def gr_half(yy, c):
         return jnp.dot(dl[yy].reshape(2 * TILE, TOK), tbuf[c], preferred_element_type=F32)
 
@@ -330,31 +321,25 @@
         for hh in range(2):
             for m in range(2):
                 top = hh * TILE + m * BLOCK
-                cs[gi, hh, m] = out[top : top + SENT].astype(BF)
+                cs[gi, hh, m] = out[top : top + BLOCK].astype(BF)
         return send(cs.at[gi], cr.at[gi], CC + gi, core_peer)
 
-    def gr_own(slot, yy):
+    def gr_sums(gi, yy):
         out = gr_half(yy, k)
-        for hh in range(2):
-            for m in range(2):
-                top = hh * TILE + m * BLOCK
-                own[slot, hh, m] = out[top : top + SENT]
-
-    of_j = (1 - h, h)
-    cc = [gr_other(0, yo)]
-    gr_own(0, yo)
-    cc[0].wait_recv()
-    y1 = []
-    for m, (at, to) in enumerate(((Y1R, y_right), (Y1L, y_left))):
-        for j, hh in enumerate(of_j):
-            y1s[m, j] = (own[0, hh, m] + cr[0, hh, m].astype(F32)).astype(BF)
-        y1.append(send(y1s.at[m], y1r.at[m], at, to))
-
-    for at, zz in ((5, z), (6, zr), (7, zl)):
-        blocks(zz, 1 - h, 3)
-        hidden.append(hidden_send(at, zz, 1 - h))
-    cc.append(gr_other(1, yr))
-    cc.append(gr_other(2, yl))
+        cc[gi].wait_recv()
+
+        def part(hh, m):
+            top = hh * TILE + m * BLOCK
+            return out[top : top + BLOCK] + cr[gi, hh, m].astype(F32)
+
+        return part
+
+    def tg_far(o):
+        tgs1[o] = tg_rows(zo, o).astype(BF)
+        return (
+            send(tgs1.at[o, pl.ds(0, 128), :], tgr1.at[0, o], G1R + o, z_right),
+            send(tgs1.at[o, pl.ds(128, 128), :], tgr1.at[1, o], G1L + o, z_left),
+        )
 
     g2 = []
 
@@ -372,71 +357,100 @@
             tgs2[d, o, pl.ds(128, 128), :] = hi.astype(BF)
             g2.append(send(tgs2.at[d, o], tgr2.at[d, o], at + o, to))
 
+    g1 = [tg_far(0)]
+
+    def far_units(i, _):
+        activate((z + i + i // 2) % 4, yo, 1 - h)
+        return 0
+
+    lax.fori_loop(0, 3, far_units, 0)
+    cc = [gr_other(0, yo)]
+    part = gr_sums(0, yo)
+    y1 = []
+    for m, (at, to) in enumerate(((Y1R, y_right), (Y1L, y_left))):
+        for hh in range(2):
+            y1s[m, hh] = part(hh, m).astype(BF)
+        y1.append(send(y1s.at[m], y1r.at[m], at, to))
+    g1.append(tg_far(1))
+
+    for at, zz in ((5, zr), (6, zl)):
+        blocks(zz, 1 - h, 3)
+        hidden.append(hidden_send(at, zz, 1 - h))
     tg_near(0)
-    gr_own(1, yr)
-    gr_own(0, yl)
+    blocks(z, 1 - h, 3)
+    hidden.append(hidden_send(7, z, 1 - h))
+    cc.append(gr_other(1, yr))
+    cc.append(gr_other(2, yl))
     y2 = []
-    for j, hh in enumerate(of_j):
-        for d, (at, to) in enumerate(((Y2R, y_right), (Y2L, y_left))):
-            if j == 0:
-                cc[1 + d].wait_recv()
-                y1[d].wait_recv()
+    for d, (yy, at, to) in enumerate(((yr, Y2R, y_right), (yl, Y2L, y_left))):
+        part = gr_sums(1 + d, yy)
+        y1[d].wait_recv()
+        for hh in range(2):
+            y2s[d, hh, d] = (part(hh, d) + y1r[d, hh].astype(F32)).astype(BF)
+            y2s[d, hh, 1 - d] = part(hh, 1 - d).astype(BF)
+        y2.append([])
+        for hh in range(2):
             for m in range(2):
-                part = own[1 - d, hh, m] + cr[1 + d, hh, m].astype(F32)
-                if m == d:
-                    part = part + y1r[d, j].astype(F32)
-                y2s[d, j, m] = part.astype(BF)
-            y2.append(send(y2s.at[d, j], y2r.at[d, j], at + j, to))
-
+                y2[d].append(send(y2s.at[d, hh, m], y2r.at[d, hh, m], at + 2 * hh + m, to))
     tg_near(1)
     cc.append(gr_other(3, y))
     for o in range(2):
         tgo[o] = tg_rows(z, o)
-    gr_own(1, y)
+    part = gr_sums(3, y)
+    for hh in range(2):
+        for m in range(2):
+            own[hh, m] = part(hh, m)
 
     g2[0].wait_recv()
     g2[1].wait_recv()
     txs[...] = (tgo[0] + tgr2[0, 0].astype(F32) + tgr2[1, 0].astype(F32)).astype(BF)
     gx = send(txs, txr, GX, x_peer)
-    cc[3].wait_recv()
-    xa = remote(xs.at[1], xr.at[1], XA, swap_here)
-    xa_self = pltpu.make_async_copy(xs.at[1], xr.at[1], ls.at[12])
-    for j, hh in enumerate(of_j):
-        y2[2 * j].wait_recv()
-        y2[2 * j + 1].wait_recv()
+    def keep(hh, m):
+        here = remote(xs.at[hh, m], xr.at[0, m], XA + m, swap_here)
+        there = remote(xs.at[hh, m], xr.at[1, m], XB + m, swap_there)
+        local = pltpu.make_async_copy(xs.at[hh, m], xr.at[0, m], ls.at[12 + m])
+
+        @pl.when(jnp.logical_and(h == hh, on_self))
+        def _():
+            local.start()
+
+        @pl.when(jnp.logical_and(h == hh, jnp.logical_not(on_self)))
+        def _():
+            here.start()
+
+        @pl.when(h != hh)
+        def _():
+            there.start()
+
+        return here, there, local
+
+    kept = []
+    for hh in range(2):
         for m in range(2):
-            part = own[1, hh, m] + cr[3, hh, m].astype(F32)
-            part = part + y2r[0, j, m].astype(F32) + y2r[1, j, m].astype(F32)
-            xs[j, m] = part.astype(BF)
-        if j == 0:
-            xb = send(xs.at[0], xr.at[0], XB, swap_there)
-
-    @pl.when(on_self)
-    def _():
-        xa_self.start()
-
-    @pl.when(jnp.logical_not(on_self))
-    def _():
-        xa.start()
-
+            y2[0][2 * hh + m].wait_recv()
+            y2[1][2 * hh + m].wait_recv()
+            total = own[hh, m] + y2r[0, hh, m].astype(F32) + y2r[1, hh, m].astype(F32)
+            xs[hh, m] = total.astype(BF)
+            kept.append(keep(hh, m))
     g2[2].wait_recv()
     g2[3].wait_recv()
     gx.wait_recv()
     tg_out[...] = (
         tgo[1] + tgr2[0, 1].astype(F32) + tgr2[1, 1].astype(F32) + txr[...].astype(F32)
     ).astype(BF)
-    xb.wait_recv()
-
-    @pl.when(on_self)
-    def _():
-        xa_self.wait()
-
-    @pl.when(jnp.logical_not(on_self))
-    def _():
-        xa.wait_recv()
-
     scale = 1.0 / 128.0
     for m in range(2):
+        here, there, local = kept[m]
+        there.wait_recv()
+
+        @pl.when(on_self)
+        def _(local=local):
+            local.wait()
+
+        @pl.when(jnp.logical_not(on_self))
+        def _(here=here):
+            here.wait_recv()
+
         gr_out[m] = (xr[0, m].astype(F32) + xr[1, m].astype(F32)) * scale
 
     for mine, cp in hidden:
@@ -445,8 +459,11 @@
 
     @pl.when(jnp.logical_not(on_self))
     def _():
-        for cp in wa + [xa]:
+        for cp in wa + [kept[0][0], kept[1][0]]:
             cp.wait_send()
+
+    kept[0][1].wait_send()
+    kept[1][1].wait_send()
 
     for cp in sent:
         cp.wait_send()
@@ -458,16 +475,16 @@
     return pl.pallas_call(
         kernel,
         out_shape=(
-            jax.ShapeDtypeStruct((2, 2, 4, SENT, TOK), BF),
+            jax.ShapeDtypeStruct((2, 2, 4, BLOCK, TOK), BF),
             jax.ShapeDtypeStruct((CHUNK, HALF), BF),
-            jax.ShapeDtypeStruct((2, SENT, HALF), F32),
+            jax.ShapeDtypeStruct((2, BLOCK, HALF), F32),
         ),
         in_specs=[vmem, vmem, vmem, hbm],
         out_specs=(hbm, vmem, vmem),
         scratch_shapes=[
             pltpu.VMEM((2, TOK, HALF), BF),
             pltpu.VMEM((2, 4, 2, 2, BLOCK, HALF), BF),
-            pltpu.VMEM((2, SENT, HALF), BF),
+            pltpu.VMEM((2, BLOCK, HALF), BF),
             pltpu.VMEM((4, 2, 2, BLOCK, TOK), BF),
             pltpu.VMEM((2, 4, BLOCK, TOK), BF),
             pltpu.VMEM((2, 4 * SHARD, TOK), BF),
@@ -478,18 +495,18 @@
             pltpu.VMEM((2, CHUNK, HALF), F32),
             pltpu.VMEM((CHUNK, HALF), BF),
             pltpu.VMEM((CHUNK, HALF), BF),
-            pltpu.VMEM((4, 2, 2, SENT, HALF), BF),
-            pltpu.VMEM((4, 2, 2, SENT, HALF), BF),
-            pltpu.VMEM((2, 2, 2, SENT, HALF), F32),
-            pltpu.VMEM((2, 2, SENT, HALF), BF),
-            pltpu.VMEM((2, 2, SENT, HALF), BF),
-            pltpu.VMEM((2, 2, 2, SENT, HALF), BF),
-            pltpu.VMEM((2, 2, 2, SENT, HALF), BF),
-            pltpu.VMEM((2, 2, SENT, HALF), BF),
-            pltpu.VMEM((2, 2, SENT, HALF), BF),
+            pltpu.VMEM((4, 2, 2, BLOCK, HALF), BF),
+            pltpu.VMEM((4, 2, 2, BLOCK, HALF), BF),
+            pltpu.VMEM((2, 2, BLOCK, HALF), F32),
+            pltpu.VMEM((2, 2, BLOCK, HALF), BF),
+            pltpu.VMEM((2, 2, BLOCK, HALF), BF),
+            pltpu.VMEM((2, 2, 2, BLOCK, HALF), BF),
+            pltpu.VMEM((2, 2, 2, BLOCK, HALF), BF),
+            pltpu.VMEM((2, 2, BLOCK, HALF), BF),
+            pltpu.VMEM((2, 2, BLOCK, HALF), BF),
             pltpu.SemaphoreType.DMA((N_SEM,)),
             pltpu.SemaphoreType.DMA((N_SEM,)),
-            pltpu.SemaphoreType.DMA((13,)),
+            pltpu.SemaphoreType.DMA((14,)),
         ],
         compiler_params=pltpu.CompilerParams(
             collective_id=0, has_side_effects=True, vmem_limit_bytes=64 * 1024 * 1024,
@@ -512,7 +529,7 @@
         merge_kernel,
         out_shape=jax.ShapeDtypeStruct((FF_TILE, TOK), BF),
         grid=(4,),
-        in_specs=[pl.BlockSpec((2, 2, 1, SENT, TOK), lambda i: (0, 0, i, 0, 0))],
+        in_specs=[pl.BlockSpec((2, 2, 1, BLOCK, TOK), lambda i: (0, 0, i, 0, 0))],
         out_specs=pl.BlockSpec((4 * SHARD, TOK), lambda i: (i, 0)),
         name="merge_hidden",
     )(hid)

time: 138 us -> 137 us (level)
  no operation moved by 1% of the time
where the time goes in v4:
time: 137 us; the launch traced here: 136 us
  Pallas kernels  134 us (98%)
  local copies, waits for them, and re-layouts  1.92 us (1%)
    pallas_call x1, Pallas kernels, fused(): pl.pallas_call(kernel, out_shape=(jax.ShapeDtypeStruct((2, 2, 4, BLOCK, T...  129 us
    pallas_call x1, Pallas kernels, merge(): pl.pallas_call(merge_kernel, out_shape=jax.ShapeDtypeStruct((FF_TILE, TOK...  4.57 us

profile of v4, /device:TPU:0, one launch (start us, length us, event | category | flops | bytes accessed | tf_op | source)
XLA Modules:
  0.0 136.5 jit_solution(17679051576118645455)
XLA Ops:
  0.6 129.4 %swiglu_grid.1 = (bf16[2,2,4,112,1024]{4,3,2,1,0:T(8,128)(2,1)}, bf16[256,1280]{1,0:T(8,128)(2,1)}, f32[2,112,1280]{2,1,0:T(8,128)}) custom-call(bf16[256,1280]{1,0:T(8,128)(2,1)} %tok_ref.1, bf16[108,1280]{1,0:T(8,128)(2,1)} %gw_ref.1, bf16[108,1280]{1,0:T(8,128)(2,1)} %uw_ref.1, bf16[1728,1024]{1,0:T(8,128)(2,1)} %bitcast.7), custom_call_target="tpu_custom_call" | custom-call | flops 28185722880 | bytes 12582912 | tf_op jit(solution)/shard_map/swiglu_grid/pallas_call | solution.py:475
  130.0 0.0 copy-start
  130.0 0.0 copy-start.1
  130.0 4.6 %merge_hidden.1 = bf16[1728,1024]{1,0:T(8,128)(2,1)} custom-call(bf16[2,2,4,112,1024]{4,3,2,1,0:T(8,128)(2,1)} %get-tuple-element.7.hid_ref), custom_call_target="tpu_custom_call" | custom-call | tf_op jit(solution)/shard_map/merge_hidden/pallas_call | solution.py:528
  134.6 0.0 copy-done
  134.6 1.1 slice_bitcast_fusion
  135.7 0.0 copy-done.1
  135.7 0.8 copy.9
Async XLA Ops:
  130.0 4.6 %copy-start = (f32[2,112,1280]{2,1,0:T(8,128)S(1)}, f32[2,112,1280]{2,1,0:T(8,128)}, u32[]{:S(2)}) copy-start(f32[2,112,1280]{2,1,0:T(8,128)} %get-tuple-element.9) | copy-start | bytes 3440644
  130.0 5.7 %copy-start.1 = (bf16[256,1280]{1,0:T(8,128)(2,1)S(1)}, bf16[256,1280]{1,0:T(8,128)(2,1)}, u32[]{:S(2)}) copy-start(bf16[256,1280]{1,0:T(8,128)(2,1)} %get-tuple-element.17) | copy-start | bytes 1966084

commit v5 on v4

--- a/solution.py
+++ b/solution.py
@@ -31,7 +31,7 @@
 W1RA, W1LA, W1RB, W1LB = [place(2) for _ in range(4)]
 W2RA, W2LA, W2RB, W2LB = [place() for _ in range(4)]
 WC = place(16)
-HD = place(8)
+HD = place(16)
 G1R, G1L, G2R, G2L = [place(2) for _ in range(4)]
 GX = place()
 CC = place(4)
@@ -154,8 +154,6 @@
         wb[0].start()
         wb[1].start()
 
-    t0 = remote(tok_ref, tok_at(l, z), T0, x_peer)
-    sent.append(t0)
 
     t1r = send(tok_ref, tok_at(l, z), T1R, z_right)
     t1l = send(tok_ref, tok_at(l, z), T1L, z_left)
@@ -175,8 +173,8 @@
     def _():
         wa_self.wait()
 
-    own_a, own_b, near_a, near_b = [], [], [], []
-    w1ra, w1la, w1rb, w1lb = [], [], [], []
+    own_a, near_a = [], []
+    w1ra, w1la = [], []
     for m in range(2):
 
         @pl.when(jnp.logical_not(on_self))
@@ -186,7 +184,38 @@
         w1ra.append(pass_on(y, h, m, W1RA + m, y_right))
         w1la.append(pass_on(y, h, m, W1LA + m, y_left))
         own_a.append(share(0, y, h, m))
-    t0.start()
+    t0 = send(tok_ref, tok_at(l, z), T0, x_peer)
+
+    def later(yy, hh, m, at, to):
+        cp = remote(piece(yy, hh, m), piece(yy, hh, m), at, to)
+        sent.append(cp)
+        return cp
+
+    w1rb = [later(y, 1 - h, m, W1RB + m, y_right) for m in range(2)]
+    w1lb = [later(y, 1 - h, m, W1LB + m, y_left) for m in range(2)]
+    own_b = [later(y, 1 - h, m, WC + 2 + m, core_peer) for m in range(2)]
+    w2rb = later(yl, 1 - h, 0, W2RB, y_right)
+    w2lb = later(yr, 1 - h, 1, W2LB, y_left)
+    left_b = [later(yl, 1 - h, m, WC + 8 + m, core_peer) for m in range(2)]
+    right_b = [later(yr, 1 - h, m, WC + 10 + m, core_peer) for m in range(2)]
+
+    def pass_own_b():
+        for m in range(2):
+            wb[m].wait_recv()
+            w1rb[m].start()
+            w1lb[m].start()
+            own_b[m].start()
+
+    def pass_near_b():
+        for m in range(2):
+            w1rb[m].wait_recv()
+            if m == 0:
+                w2rb.start()
+            left_b[m].start()
+            w1lb[m].wait_recv()
+            if m == 1:
+                w2lb.start()
+            right_b[m].start()
 
     def spread(i, _):
         raw_copy(i).wait()
@@ -207,6 +236,10 @@
         return 0
 
     lax.fori_loop(0, 4, spread, 0)
+
+    @pl.when(jnp.logical_not(on_self))
+    def _():
+        pass_own_b()
 
     t1r.wait_recv()
     t3r = send(tok_half(l, zl, 0), tok_half(l, zl, 0), T3R, z_right)
@@ -230,23 +263,19 @@
         wb[0].start()
         wb[1].start()
 
-    t3r.wait_recv()
-    t3l.wait_recv()
-    for m in range(2):
-        wb[m].wait_recv()
-        w1rb.append(pass_on(y, 1 - h, m, W1RB + m, y_right))
-        w1lb.append(pass_on(y, 1 - h, m, W1LB + m, y_left))
-        own_b.append(share(1, y, 1 - h, m))
+    @pl.when(jnp.logical_not(on_self))
+    def _():
+        pass_near_b()
+
     w2ra.wait_recv()
     far_a = [share(6, yo, h, 0)]
     w2la.wait_recv()
     far_a.append(share(6, yo, h, 1))
+    t3r.wait_recv()
+    t3l.wait_recv()
     t_self.wait()
 
-    def activate(zz, yy, hh):
-        cols = at_rows(zz)
-        gu = rows_by_rows(wbuf[0, yy, hh].reshape(TILE, HALF), tbuf[0, cols, :])
-        gu += rows_by_rows(wbuf[1, yy, hh].reshape(TILE, HALF), tbuf[1, cols, :])
+    def finish(gu, yy, hh, cols):
         gate, up = gu[:BLOCK], gu[BLOCK:]
         back = dl[yy, hh, 0, :, cols].astype(F32)
         s = jax.nn.sigmoid(gate)
@@ -255,57 +284,81 @@
         dl[yy, hh, 0, :, cols] = (back * up * s * (1.0 + gate * (1.0 - s))).astype(BF)
         dl[yy, hh, 1, :, cols] = (back * gs).astype(BF)
 
-    def blocks(zz, hh, count):
-        def step(i, _):
-            activate(zz, (y + i + i // 2 - 2 * (i // 3)) % 4, hh)
-            return 0
-
-        lax.fori_loop(0, count, step, 0)
-
-    def hidden_send(at, zz, hh):
-        part = hid.at[hh, :, :, at_rows(zz)]
-        there = hid_out.at[l, hh, :, :, at_rows(zz)]
-        mine = pltpu.make_async_copy(part, there, ls.at[4 + at])
-        mine.start()
-        return mine, send(part, there, HD + at, x_peer)
+    def hidden_copy(at, zz, yy):
+        part = hid.at[:, yy, :, at_rows(zz)]
+        return remote(part, hid_out.at[l, :, yy, :, at_rows(zz)], HD + at, x_peer)
+
+    def one_block(zz, yy, hh):
+        cols = at_rows(zz)
+        gu = rows_by_rows(wbuf[0, yy, hh].reshape(TILE, HALF), tbuf[0, cols, :])
+        gu += rows_by_rows(wbuf[1, yy, hh].reshape(TILE, HALF), tbuf[1, cols, :])
+        finish(gu, yy, hh, cols)
+
+    def two_blocks(at, zz, yy):
+        cols = at_rows(zz)
+        gu = rows_by_rows(wbuf[0, yy].reshape(2 * TILE, HALF), tbuf[0, cols, :])
+        gu += rows_by_rows(wbuf[1, yy].reshape(2 * TILE, HALF), tbuf[1, cols, :])
+        for hh in range(2):
+            finish(gu[hh * TILE : (hh + 1) * TILE], yy, hh, cols)
+        hidden_copy(at, zz, yy).start()
+
+    def place_of(i, start):
+        return (start + i + i // 2 - 2 * (i // 3)) % 4
 
     def arrived(copies):
         for cp in copies:
             cp.wait_recv()
 
     arrived(own_a + near_a + far_a)
-    blocks(z, h, 4)
-    hidden = [hidden_send(0, z, h)]
+
+    def first(i, _):
+        one_block(z, place_of(i, y), h)
+        return 0
+
+    lax.fori_loop(0, 4, first, 0)
+
+    @pl.when(on_self)
+    def _():
+        pass_own_b()
+        pass_near_b()
+
     t2r.wait_recv()
     t4r = send(tok_half(1 - l, zl, 0), tok_half(1 - l, zl, 0), T4R, z_right)
     t2l.wait_recv()
     t4l = send(tok_half(1 - l, zr, 1), tok_half(1 - l, zr, 1), T4L, z_left)
-    blocks(zl, h, 4)
-    hidden.append(hidden_send(1, zl, h))
-    for m in range(2):
-        w1rb[m].wait_recv()
-        if m == 0:
-            w2rb = pass_on(yl, 1 - h, 0, W2RB, y_right)
-        near_b.append(share(4, yl, 1 - h, m))
-        w1lb[m].wait_recv()
-        if m == 1:
-            w2lb = pass_on(yr, 1 - h, 1, W2LB, y_left)
-        near_b.append(share(5, yr, 1 - h, m))
-    blocks(zr, h, 4)
-    hidden.append(hidden_send(2, zr, h))
-    t4r.wait_recv()
-    t4l.wait_recv()
-    blocks(zo, h, 4)
-    hidden.append(hidden_send(3, zo, h))
-    arrived(own_b + near_b)
-    blocks(zo, 1 - h, 3)
+    arrived(own_b + left_b + right_b)
+
+    def second(i, _):
+        yy = place_of(i, y)
+        one_block(z, yy, 1 - h)
+        hidden_copy(i, z, yy).start()
+        return 0
+
+    def near_units(zi):
+        def step(i, _):
+            two_blocks(4 * zi + i, place_of(zi, z), place_of(i, y))
+            return 0
+
+        lax.fori_loop(0, 3, step, 0)
+
+    lax.fori_loop(0, 3, second, 0)
+    near_units(1)
     w2rb.wait_recv()
     far_b = [share(7, yo, 1 - h, 0)]
     w2lb.wait_recv()
     far_b.append(share(7, yo, 1 - h, 1))
+    near_units(2)
     arrived(far_b)
-    activate(zo, yo, 1 - h)
-    hidden.append(hidden_send(4, zo, 1 - h))
+    lax.fori_loop(3, 4, second, 0)
+
+    def far_units(i, _):
+        two_blocks(4 * i + 3, place_of(i, z), yo)
+        return 0
+
+    lax.fori_loop(1, 3, far_units, 0)
+    t4r.wait_recv()
+    t4l.wait_recv()
+    two_blocks(15, zo, yo)
 
     def tg_rows(zz, o):
         c = (1 - l) if o == 0 else l
@@ -333,6 +386,12 @@
             return out[top : top + BLOCK] + cr[gi, hh, m].astype(F32)
 
         return part
+
+    def gr_own(slot, gi, yy):
+        part = gr_sums(gi, yy)
+        for hh in range(2):
+            for m in range(2):
+                own[slot, hh, m] = part(hh, m)
 
     def tg_far(o):
         tgs1[o] = tg_rows(zo, o).astype(BF)
@@ -357,14 +416,11 @@
             tgs2[d, o, pl.ds(128, 128), :] = hi.astype(BF)
             g2.append(send(tgs2.at[d, o], tgr2.at[d, o], at + o, to))
 
+    cc = [gr_other(0, yo)]
+    near_units(3)
+    mine = pltpu.make_async_copy(hid, hid_out.at[l], ls.at[4])
+    mine.start()
     g1 = [tg_far(0)]
-
-    def far_units(i, _):
-        activate((z + i + i // 2) % 4, yo, 1 - h)
-        return 0
-
-    lax.fori_loop(0, 3, far_units, 0)
-    cc = [gr_other(0, yo)]
     part = gr_sums(0, yo)
     y1 = []
     for m, (at, to) in enumerate(((Y1R, y_right), (Y1L, y_left))):
@@ -372,34 +428,27 @@
             y1s[m, hh] = part(hh, m).astype(BF)
         y1.append(send(y1s.at[m], y1r.at[m], at, to))
     g1.append(tg_far(1))
-
-    for at, zz in ((5, zr), (6, zl)):
-        blocks(zz, 1 - h, 3)
-        hidden.append(hidden_send(at, zz, 1 - h))
-    tg_near(0)
-    blocks(z, 1 - h, 3)
-    hidden.append(hidden_send(7, z, 1 - h))
     cc.append(gr_other(1, yr))
     cc.append(gr_other(2, yl))
+    tg_near(0)
+    gr_own(0, 1, yr)
+    gr_own(1, 2, yl)
     y2 = []
-    for d, (yy, at, to) in enumerate(((yr, Y2R, y_right), (yl, Y2L, y_left))):
-        part = gr_sums(1 + d, yy)
+    for d, (at, to) in enumerate(((Y2R, y_right), (Y2L, y_left))):
         y1[d].wait_recv()
-        for hh in range(2):
-            y2s[d, hh, d] = (part(hh, d) + y1r[d, hh].astype(F32)).astype(BF)
-            y2s[d, hh, 1 - d] = part(hh, 1 - d).astype(BF)
         y2.append([])
         for hh in range(2):
             for m in range(2):
+                total = own[d, hh, m]
+                if m == d:
+                    total = total + y1r[d, hh].astype(F32)
+                y2s[d, hh, m] = total.astype(BF)
                 y2[d].append(send(y2s.at[d, hh, m], y2r.at[d, hh, m], at + 2 * hh + m, to))
     tg_near(1)
-    cc.append(gr_other(3, y))
     for o in range(2):
         tgo[o] = tg_rows(z, o)
-    part = gr_sums(3, y)
-    for hh in range(2):
-        for m in range(2):
-            own[hh, m] = part(hh, m)
+    cc.append(gr_other(3, y))
+    gr_own(0, 3, y)
 
     g2[0].wait_recv()
     g2[1].wait_recv()
@@ -408,7 +457,7 @@
     def keep(hh, m):
         here = remote(xs.at[hh, m], xr.at[0, m], XA + m, swap_here)
         there = remote(xs.at[hh, m], xr.at[1, m], XB + m, swap_there)
-        local = pltpu.make_async_copy(xs.at[hh, m], xr.at[0, m], ls.at[12 + m])
+        local = pltpu.make_async_copy(xs.at[hh, m], xr.at[0, m], ls.at[5 + m])
 
         @pl.when(jnp.logical_and(h == hh, on_self))
         def _():
@@ -429,7 +478,7 @@
         for m in range(2):
             y2[0][2 * hh + m].wait_recv()
             y2[1][2 * hh + m].wait_recv()
-            total = own[hh, m] + y2r[0, hh, m].astype(F32) + y2r[1, hh, m].astype(F32)
+            total = own[0, hh, m] + y2r[0, hh, m].astype(F32) + y2r[1, hh, m].astype(F32)
             xs[hh, m] = total.astype(BF)
             kept.append(keep(hh, m))
     g2[2].wait_recv()
@@ -453,9 +502,15 @@
 
         gr_out[m] = (xr[0, m].astype(F32) + xr[1, m].astype(F32)) * scale
 
-    for mine, cp in hidden:
-        mine.wait()
+    mine.wait()
+
+    def hidden_done(i, _):
+        cp = hidden_copy(i, 0, 0)
         cp.wait_recv()
+        cp.wait_send()
+        return 0
+
+    lax.fori_loop(0, 16, hidden_done, 0)
 
     @pl.when(jnp.logical_not(on_self))
     def _():
@@ -497,7 +552,7 @@
             pltpu.VMEM((CHUNK, HALF), BF),
             pltpu.VMEM((4, 2, 2, BLOCK, HALF), BF),
             pltpu.VMEM((4, 2, 2, BLOCK, HALF), BF),
-            pltpu.VMEM((2, 2, BLOCK, HALF), F32),
+            pltpu.VMEM((2, 2, 2, BLOCK, HALF), F32),
             pltpu.VMEM((2, 2, BLOCK, HALF), BF),
             pltpu.VMEM((2, 2, BLOCK, HALF), BF),
             pltpu.VMEM((2, 2, 2, BLOCK, HALF), BF),
@@ -506,7 +561,7 @@
             pltpu.VMEM((2, 2, BLOCK, HALF), BF),
             pltpu.SemaphoreType.DMA((N_SEM,)),
             pltpu.SemaphoreType.DMA((N_SEM,)),
-            pltpu.SemaphoreType.DMA((14,)),
+            pltpu.SemaphoreType.DMA((7,)),
         ],
         compiler_params=pltpu.CompilerParams(
             collective_id=0, has_side_effects=True, vmem_limit_bytes=64 * 1024 * 1024,

time: 137 us -> 142 us (1.036)
  Pallas kernels: 134 us -> 139 us
    pallas_call x1, Pallas kernels: 129 us -> 135 us  [fused(): pl.pallas_call(kernel, out_shape=(jax.ShapeDtypeStruct((2, 2, 4, BLOCK, T...]
where the time goes in v5:
time: 142 us
  Pallas kernels  139 us (98%)
  local copies, waits for them, and re-layouts  1.92 us (1%)
    pallas_call x1, Pallas kernels, fused(): pl.pallas_call(kernel, out_shape=(jax.ShapeDtypeStruct((2, 2, 4, BLOCK, T...  135 us
    pallas_call x1, Pallas kernels, merge(): pl.pallas_call(merge_kernel, out_shape=jax.ShapeDtypeStruct((FF_TILE, TOK...  4.57 us

profile of v5, /device:TPU:0, one launch (start us, length us, event | category | flops | bytes accessed | tf_op | source)
XLA Modules:
  0.0 142.0 jit_solution(12030023948953985859)
XLA Ops:
  0.6 134.9 %swiglu_grid.1 = (bf16[2,2,4,112,1024]{4,3,2,1,0:T(8,128)(2,1)}, bf16[256,1280]{1,0:T(8,128)(2,1)}, f32[2,112,1280]{2,1,0:T(8,128)}) custom-call(bf16[256,1280]{1,0:T(8,128)(2,1)} %tok_ref.1, bf16[108,1280]{1,0:T(8,128)(2,1)} %gw_ref.1, bf16[108,1280]{1,0:T(8,128)(2,1)} %uw_ref.1, bf16[1728,1024]{1,0:T(8,128)(2,1)} %bitcast.7), custom_call_target="tpu_custom_call" | custom-call | flops 28185722880 | bytes 12582912 | tf_op jit(solution)/shard_map/swiglu_grid/pallas_call | solution.py:530
  135.5 0.0 copy-start
  135.6 0.0 copy-start.1
  135.6 4.6 %merge_hidden.1 = bf16[1728,1024]{1,0:T(8,128)(2,1)} custom-call(bf16[2,2,4,112,1024]{4,3,2,1,0:T(8,128)(2,1)} %get-tuple-element.7.hid_ref), custom_call_target="tpu_custom_call" | custom-call | tf_op jit(solution)/shard_map/merge_hidden/pallas_call | solution.py:583
  140.1 0.0 copy-done
  140.1 1.1 slice_bitcast_fusion
  141.2 0.0 copy-done.1
  141.2 0.8 copy.9
Async XLA Ops:
  135.5 4.6 %copy-start = (f32[2,112,1280]{2,1,0:T(8,128)S(1)}, f32[2,112,1280]{2,1,0:T(8,128)}, u32[]{:S(2)}) copy-start(f32[2,112,1280]{2,1,0:T(8,128)} %get-tuple-element.9) | copy-start | bytes 3440644
  135.6 5.7 %copy-start.1 = (bf16[256,1280]{1,0:T(8,128)(2,1)S(1)}, bf16[256,1280]{1,0:T(8,128)(2,1)}, u32[]{:S(2)}) copy-start(bf16[256,1280]{1,0:T(8,128)(2,1)} %get-tuple-element.17) | copy-start | bytes 1966084

commit v6 on v5

--- a/solution.py
+++ b/solution.py
@@ -320,12 +320,16 @@
     @pl.when(on_self)
     def _():
         pass_own_b()
-        pass_near_b()
 
     t2r.wait_recv()
     t4r = send(tok_half(1 - l, zl, 0), tok_half(1 - l, zl, 0), T4R, z_right)
     t2l.wait_recv()
     t4l = send(tok_half(1 - l, zr, 1), tok_half(1 - l, zr, 1), T4L, z_left)
+
+    @pl.when(on_self)
+    def _():
+        pass_near_b()
+
     arrived(own_b + left_b + right_b)
 
     def second(i, _):
@@ -414,7 +418,9 @@
                 hi = hi + far
             tgs2[d, o, pl.ds(0, 128), :] = lo.astype(BF)
             tgs2[d, o, pl.ds(128, 128), :] = hi.astype(BF)
-            g2.append(send(tgs2.at[d, o], tgr2.at[d, o], at + o, to))
+            g2.append(remote(tgs2.at[d, o], tgr2.at[d, o], at + o, to))
+            if o == 0:
+                g2[d].start()
 
     cc = [gr_other(0, yo)]
     near_units(3)
@@ -443,44 +449,63 @@
                 if m == d:
                     total = total + y1r[d, hh].astype(F32)
                 y2s[d, hh, m] = total.astype(BF)
-                y2[d].append(send(y2s.at[d, hh, m], y2r.at[d, hh, m], at + 2 * hh + m, to))
+                cp = remote(y2s.at[d, hh, m], y2r.at[d, hh, m], at + 2 * hh + m, to)
+                if hh == 0:
+                    cp.start()
+                y2[d].append(cp)
     tg_near(1)
-    for o in range(2):
-        tgo[o] = tg_rows(z, o)
+    tgo[0] = tg_rows(z, 0)
     cc.append(gr_other(3, y))
+    tgo[1] = tg_rows(z, 1)
+    for d in range(2):
+        g2[d].wait_send()
+        g2[2 + d].start()
     gr_own(0, 3, y)
 
+    def keep(hh, m):
+        here = remote(xs.at[hh, m], xr.at[0, m], XA + m, swap_here)
+        there = remote(xs.at[hh, m], xr.at[1, m], XB + m, swap_there)
+        local = pltpu.make_async_copy(xs.at[hh, m], xr.at[0, m], ls.at[5 + m])
+
+        @pl.when(jnp.logical_and(h == hh, on_self))
+        def _():
+            local.start()
+
+        @pl.when(jnp.logical_and(h == hh, jnp.logical_not(on_self)))
+        def _():
+            here.start()
+
+        @pl.when(h != hh)
+        def _():
+            there.start()
+
+        return here, there, local
+
+    def next_piece(m, before):
+        for d in range(2):
+            for at in before:
+                y2[d][at].wait_send()
+            y2[d][2 + m].start()
+
+    kept = []
+
+    def keep_sum(hh, m):
+        y2[0][2 * hh + m].wait_recv()
+        y2[1][2 * hh + m].wait_recv()
+        total = own[0, hh, m] + y2r[0, hh, m].astype(F32) + y2r[1, hh, m].astype(F32)
+        xs[hh, m] = total.astype(BF)
+        kept.append(keep(hh, m))
+
+    next_piece(0, (0, 1))
     g2[0].wait_recv()
     g2[1].wait_recv()
     txs[...] = (tgo[0] + tgr2[0, 0].astype(F32) + tgr2[1, 0].astype(F32)).astype(BF)
     gx = send(txs, txr, GX, x_peer)
-    def keep(hh, m):
-        here = remote(xs.at[hh, m], xr.at[0, m], XA + m, swap_here)
-        there = remote(xs.at[hh, m], xr.at[1, m], XB + m, swap_there)
-        local = pltpu.make_async_copy(xs.at[hh, m], xr.at[0, m], ls.at[5 + m])
-
-        @pl.when(jnp.logical_and(h == hh, on_self))
-        def _():
-            local.start()
-
-        @pl.when(jnp.logical_and(h == hh, jnp.logical_not(on_self)))
-        def _():
-            here.start()
-
-        @pl.when(h != hh)
-        def _():
-            there.start()
-
-        return here, there, local
-
-    kept = []
-    for hh in range(2):
-        for m in range(2):
-            y2[0][2 * hh + m].wait_recv()
-            y2[1][2 * hh + m].wait_recv()
-            total = own[0, hh, m] + y2r[0, hh, m].astype(F32) + y2r[1, hh, m].astype(F32)
-            xs[hh, m] = total.astype(BF)
-            kept.append(keep(hh, m))
+    keep_sum(0, 0)
+    keep_sum(0, 1)
+    next_piece(1, (2,))
+    keep_sum(1, 0)
+    keep_sum(1, 1)
     g2[2].wait_recv()
     g2[3].wait_recv()
     gx.wait_recv()
@@ -520,7 +545,7 @@
     kept[0][1].wait_send()
     kept[1][1].wait_send()
 
-    for cp in sent:
+    for cp in sent + g2[2:] + [y2[0][3], y2[1][3]]:
         cp.wait_send()
 
 

time: 142 us -> 142 us (level)
  no operation moved by 1% of the time
where the time goes in v6:
time: 142 us; the launch traced here: 141 us
  Pallas kernels  139 us (98%)
  local copies, waits for them, and re-layouts  1.92 us (1%)
    pallas_call x1, Pallas kernels, fused(): pl.pallas_call(kernel, out_shape=(jax.ShapeDtypeStruct((2, 2, 4, BLOCK, T...  134 us
    pallas_call x1, Pallas kernels, merge(): pl.pallas_call(merge_kernel, out_shape=jax.ShapeDtypeStruct((FF_TILE, TOK...  4.57 us

profile of v6, /device:TPU:0, one launch (start us, length us, event | category | flops | bytes accessed | tf_op | source)
XLA Modules:
  0.0 141.5 jit_solution(2954753645761902870)
XLA Ops:
  0.6 134.4 %swiglu_grid.1 = (bf16[2,2,4,112,1024]{4,3,2,1,0:T(8,128)(2,1)}, bf16[256,1280]{1,0:T(8,128)(2,1)}, f32[2,112,1280]{2,1,0:T(8,128)}) custom-call(bf16[256,1280]{1,0:T(8,128)(2,1)} %tok_ref.1, bf16[108,1280]{1,0:T(8,128)(2,1)} %gw_ref.1, bf16[108,1280]{1,0:T(8,128)(2,1)} %uw_ref.1, bf16[1728,1024]{1,0:T(8,128)(2,1)} %bitcast.7), custom_call_target="tpu_custom_call" | custom-call | flops 28185722880 | bytes 12582912 | tf_op jit(solution)/shard_map/swiglu_grid/pallas_call | solution.py:555
  135.0 0.0 copy-start
  135.0 0.0 copy-start.1
  135.0 4.6 %merge_hidden.1 = bf16[1728,1024]{1,0:T(8,128)(2,1)} custom-call(bf16[2,2,4,112,1024]{4,3,2,1,0:T(8,128)(2,1)} %get-tuple-element.7.hid_ref), custom_call_target="tpu_custom_call" | custom-call | tf_op jit(solution)/shard_map/merge_hidden/pallas_call | solution.py:608
  139.6 0.0 copy-done
  139.6 1.1 slice_bitcast_fusion
  140.7 0.0 copy-done.1
  140.7 0.8 copy.9
Async XLA Ops:
  135.0 4.6 %copy-start = (f32[2,112,1280]{2,1,0:T(8,128)S(1)}, f32[2,112,1280]{2,1,0:T(8,128)}, u32[]{:S(2)}) copy-start(f32[2,112,1280]{2,1,0:T(8,128)} %get-tuple-element.9) | copy-start | bytes 3440644
  135.0 5.7 %copy-start.1 = (bf16[256,1280]{1,0:T(8,128)(2,1)S(1)}, bf16[256,1280]{1,0:T(8,128)(2,1)}, u32[]{:S(2)}) copy-start(bf16[256,1280]{1,0:T(8,128)(2,1)} %get-tuple-element.17) | copy-start | bytes 1966084

commit v7 on v6

--- a/solution.py
+++ b/solution.py
@@ -311,11 +311,14 @@
 
     arrived(own_a + near_a + far_a)
 
-    def first(i, _):
-        one_block(z, place_of(i, y), h)
-        return 0
-
-    lax.fori_loop(0, 4, first, 0)
+    def first_blocks(zz):
+        def step(i, _):
+            one_block(zz, place_of(i, y), h)
+            return 0
+
+        lax.fori_loop(0, 4, step, 0)
+
+    first_blocks(z)
 
     @pl.when(on_self)
     def _():
@@ -330,13 +333,17 @@
     def _():
         pass_near_b()
 
+    first_blocks(zl)
     arrived(own_b + left_b + right_b)
 
-    def second(i, _):
-        yy = place_of(i, y)
-        one_block(z, yy, 1 - h)
-        hidden_copy(i, z, yy).start()
-        return 0
+    def second_blocks(zi, start, end):
+        def step(i, _):
+            zz, yy = place_of(zi, z), place_of(i, y)
+            one_block(zz, yy, 1 - h)
+            hidden_copy(4 * zi + i, zz, yy).start()
+            return 0
+
+        lax.fori_loop(start, end, step, 0)
 
     def near_units(zi):
         def step(i, _):
@@ -345,21 +352,17 @@
 
         lax.fori_loop(0, 3, step, 0)
 
-    lax.fori_loop(0, 3, second, 0)
-    near_units(1)
+    second_blocks(0, 0, 3)
+    second_blocks(2, 0, 3)
     w2rb.wait_recv()
     far_b = [share(7, yo, 1 - h, 0)]
     w2lb.wait_recv()
     far_b.append(share(7, yo, 1 - h, 1))
-    near_units(2)
+    near_units(1)
     arrived(far_b)
-    lax.fori_loop(3, 4, second, 0)
-
-    def far_units(i, _):
-        two_blocks(4 * i + 3, place_of(i, z), yo)
-        return 0
-
-    lax.fori_loop(1, 3, far_units, 0)
+    second_blocks(0, 3, 4)
+    second_blocks(2, 3, 4)
+    two_blocks(7, zr, yo)
     t4r.wait_recv()
     t4l.wait_recv()
     two_blocks(15, zo, yo)
@@ -433,53 +436,39 @@
         for hh in range(2):
             y1s[m, hh] = part(hh, m).astype(BF)
         y1.append(send(y1s.at[m], y1r.at[m], at, to))
+    tg_near(0)
     g1.append(tg_far(1))
     cc.append(gr_other(1, yr))
     cc.append(gr_other(2, yl))
-    tg_near(0)
     gr_own(0, 1, yr)
     gr_own(1, 2, yl)
+    of_j = (1 - h, h)
     y2 = []
     for d, (at, to) in enumerate(((Y2R, y_right), (Y2L, y_left))):
         y1[d].wait_recv()
         y2.append([])
-        for hh in range(2):
+        for j, hh in enumerate(of_j):
             for m in range(2):
                 total = own[d, hh, m]
                 if m == d:
                     total = total + y1r[d, hh].astype(F32)
-                y2s[d, hh, m] = total.astype(BF)
-                cp = remote(y2s.at[d, hh, m], y2r.at[d, hh, m], at + 2 * hh + m, to)
-                if hh == 0:
+                y2s[d, j, m] = total.astype(BF)
+                cp = remote(y2s.at[d, j, m], y2r.at[d, j, m], at + 2 * j + m, to)
+                if j == 0:
                     cp.start()
                 y2[d].append(cp)
     tg_near(1)
-    tgo[0] = tg_rows(z, 0)
+    mine_other = tg_rows(z, 0)
+    g2[0].wait_recv()
+    g2[1].wait_recv()
+    txs[...] = (mine_other + tgr2[0, 0].astype(F32) + tgr2[1, 0].astype(F32)).astype(BF)
+    gx = send(txs, txr, GX, x_peer)
     cc.append(gr_other(3, y))
-    tgo[1] = tg_rows(z, 1)
+    tgo[...] = tg_rows(z, 1)
     for d in range(2):
         g2[d].wait_send()
         g2[2 + d].start()
     gr_own(0, 3, y)
-
-    def keep(hh, m):
-        here = remote(xs.at[hh, m], xr.at[0, m], XA + m, swap_here)
-        there = remote(xs.at[hh, m], xr.at[1, m], XB + m, swap_there)
-        local = pltpu.make_async_copy(xs.at[hh, m], xr.at[0, m], ls.at[5 + m])
-
-        @pl.when(jnp.logical_and(h == hh, on_self))
-        def _():
-            local.start()
-
-        @pl.when(jnp.logical_and(h == hh, jnp.logical_not(on_self)))
-        def _():
-            here.start()
-
-        @pl.when(h != hh)
-        def _():
-            there.start()
-
-        return here, there, local
 
     def next_piece(m, before):
         for d in range(2):
@@ -487,20 +476,28 @@
                 y2[d][at].wait_send()
             y2[d][2 + m].start()
 
-    kept = []
-
-    def keep_sum(hh, m):
-        y2[0][2 * hh + m].wait_recv()
-        y2[1][2 * hh + m].wait_recv()
-        total = own[0, hh, m] + y2r[0, hh, m].astype(F32) + y2r[1, hh, m].astype(F32)
-        xs[hh, m] = total.astype(BF)
-        kept.append(keep(hh, m))
+    here = [remote(xs.at[1, m], xr.at[1, m], XA + m, swap_here) for m in range(2)]
+    there = [remote(xs.at[0, m], xr.at[0, m], XB + m, swap_there) for m in range(2)]
+    local = [pltpu.make_async_copy(xs.at[1, m], xr.at[1, m], ls.at[5 + m]) for m in range(2)]
+
+    def keep_sum(j, m):
+        y2[0][2 * j + m].wait_recv()
+        y2[1][2 * j + m].wait_recv()
+        total = own[0, of_j[j], m] + y2r[0, j, m].astype(F32) + y2r[1, j, m].astype(F32)
+        xs[j, m] = total.astype(BF)
+        if j == 0:
+            there[m].start()
+        else:
+
+            @pl.when(on_self)
+            def _():
+                local[m].start()
+
+            @pl.when(jnp.logical_not(on_self))
+            def _():
+                here[m].start()
 
     next_piece(0, (0, 1))
-    g2[0].wait_recv()
-    g2[1].wait_recv()
-    txs[...] = (tgo[0] + tgr2[0, 0].astype(F32) + tgr2[1, 0].astype(F32)).astype(BF)
-    gx = send(txs, txr, GX, x_peer)
     keep_sum(0, 0)
     keep_sum(0, 1)
     next_piece(1, (2,))
@@ -510,20 +507,19 @@
     g2[3].wait_recv()
     gx.wait_recv()
     tg_out[...] = (
-        tgo[1] + tgr2[0, 1].astype(F32) + tgr2[1, 1].astype(F32) + txr[...].astype(F32)
+        tgo[...] + tgr2[0, 1].astype(F32) + tgr2[1, 1].astype(F32) + txr[...].astype(F32)
     ).astype(BF)
     scale = 1.0 / 128.0
     for m in range(2):
-        here, there, local = kept[m]
-        there.wait_recv()
+        there[m].wait_recv()
 
         @pl.when(on_self)
-        def _(local=local):
-            local.wait()
+        def _(m=m):
+            local[m].wait()
 
         @pl.when(jnp.logical_not(on_self))
-        def _(here=here):
-            here.wait_recv()
+        def _(m=m):
+            here[m].wait_recv()
 
         gr_out[m] = (xr[0, m].astype(F32) + xr[1, m].astype(F32)) * scale
 
@@ -539,13 +535,11 @@
 
     @pl.when(jnp.logical_not(on_self))
     def _():
-        for cp in wa + [kept[0][0], kept[1][0]]:
+        for cp in wa + here:
             cp.wait_send()
 
-    kept[0][1].wait_send()
-    kept[1][1].wait_send()
-
-    for cp in sent + g2[2:] + [y2[0][3], y2[1][3]]:
+
+    for cp in sent + g2[2:] + there + [y2[0][3], y2[1][3]]:
         cp.wait_send()
 
 
@@ -572,7 +566,7 @@
             pltpu.VMEM((2, 2, 128, HALF), BF),
             pltpu.VMEM((2, 2, CHUNK, HALF), BF),
             pltpu.VMEM((2, 2, CHUNK, HALF), BF),
-            pltpu.VMEM((2, CHUNK, HALF), F32),
+            pltpu.VMEM((CHUNK, HALF), F32),
             pltpu.VMEM((CHUNK, HALF), BF),
             pltpu.VMEM((CHUNK, HALF), BF),
             pltpu.VMEM((4, 2, 2, BLOCK, HALF), BF),

time: 142 us -> 145 us (1.021)
  Pallas kernels: 139 us -> 142 us
    pallas_call x1, Pallas kernels: 134 us -> 137 us  [fused(): pl.pallas_call(kernel, out_shape=(jax.ShapeDtypeStruct((2, 2, 4, BLOCK, T...]
where the time goes in v7:
time: 145 us; the launch traced here: 144 us
  Pallas kernels  142 us (98%)
  local copies, waits for them, and re-layouts  1.92 us (1%)
    pallas_call x1, Pallas kernels, fused(): pl.pallas_call(kernel, out_shape=(jax.ShapeDtypeStruct((2, 2, 4, BLOCK, T...  137 us
    pallas_call x1, Pallas kernels, merge(): pl.pallas_call(merge_kernel, out_shape=jax.ShapeDtypeStruct((FF_TILE, TOK...  4.57 us

profile of v7, /device:TPU:0, one launch (start us, length us, event | category | flops | bytes accessed | tf_op | source)
XLA Modules:
  0.0 144.2 jit_solution(8011390110087164892)
XLA Ops:
  0.6 137.1 %swiglu_grid.1 = (bf16[2,2,4,112,1024]{4,3,2,1,0:T(8,128)(2,1)}, bf16[256,1280]{1,0:T(8,128)(2,1)}, f32[2,112,1280]{2,1,0:T(8,128)}) custom-call(bf16[256,1280]{1,0:T(8,128)(2,1)} %tok_ref.1, bf16[108,1280]{1,0:T(8,128)(2,1)} %gw_ref.1, bf16[108,1280]{1,0:T(8,128)(2,1)} %uw_ref.1, bf16[1728,1024]{1,0:T(8,128)(2,1)} %bitcast.7), custom_call_target="tpu_custom_call" | custom-call | flops 28185722880 | bytes 12582912 | tf_op jit(solution)/shard_map/swiglu_grid/pallas_call | solution.py:549
  137.7 0.0 copy-start
  137.7 0.0 copy-start.1
  137.7 4.6 %merge_hidden.1 = bf16[1728,1024]{1,0:T(8,128)(2,1)} custom-call(bf16[2,2,4,112,1024]{4,3,2,1,0:T(8,128)(2,1)} %get-tuple-element.7.hid_ref), custom_call_target="tpu_custom_call" | custom-call | tf_op jit(solution)/shard_map/merge_hidden/pallas_call | solution.py:602
  142.3 0.0 copy-done
  142.3 1.1 slice_bitcast_fusion
  143.4 0.0 copy-done.1
  143.4 0.8 copy.9
Async XLA Ops:
  137.7 4.6 %copy-start = (f32[2,112,1280]{2,1,0:T(8,128)S(1)}, f32[2,112,1280]{2,1,0:T(8,128)}, u32[]{:S(2)}) copy-start(f32[2,112,1280]{2,1,0:T(8,128)} %get-tuple-element.9) | copy-start | bytes 3440644
  137.7 5.7 %copy-start.1 = (bf16[256,1280]{1,0:T(8,128)(2,1)S(1)}, bf16[256,1280]{1,0:T(8,128)(2,1)}, u32[]{:S(2)}) copy-start(bf16[256,1280]{1,0:T(8,128)(2,1)} %get-tuple-element.17) | copy-start | bytes 1966084

commit v8 on v7

--- a/solution.py
+++ b/solution.py
@@ -334,6 +334,7 @@
         pass_near_b()
 
     first_blocks(zl)
+    first_blocks(zr)
     arrived(own_b + left_b + right_b)
 
     def second_blocks(zi, start, end):
@@ -352,19 +353,14 @@
 
         lax.fori_loop(0, 3, step, 0)
 
-    second_blocks(0, 0, 3)
-    second_blocks(2, 0, 3)
     w2rb.wait_recv()
     far_b = [share(7, yo, 1 - h, 0)]
     w2lb.wait_recv()
     far_b.append(share(7, yo, 1 - h, 1))
-    near_units(1)
-    arrived(far_b)
-    second_blocks(0, 3, 4)
-    second_blocks(2, 3, 4)
-    two_blocks(7, zr, yo)
     t4r.wait_recv()
     t4l.wait_recv()
+    near_units(3)
+    arrived(far_b)
     two_blocks(15, zo, yo)
 
     def tg_rows(zz, o):
@@ -425,19 +421,23 @@
             if o == 0:
                 g2[d].start()
 
+    g1 = [tg_far(0)]
+    for zi in range(3):
+        second_blocks(zi, 3, 4)
     cc = [gr_other(0, yo)]
-    near_units(3)
-    mine = pltpu.make_async_copy(hid, hid_out.at[l], ls.at[4])
-    mine.start()
-    g1 = [tg_far(0)]
     part = gr_sums(0, yo)
     y1 = []
     for m, (at, to) in enumerate(((Y1R, y_right), (Y1L, y_left))):
         for hh in range(2):
             y1s[m, hh] = part(hh, m).astype(BF)
         y1.append(send(y1s.at[m], y1r.at[m], at, to))
+    g1.append(tg_far(1))
+    second_blocks(1, 0, 3)
+    second_blocks(2, 0, 3)
     tg_near(0)
-    g1.append(tg_far(1))
+    second_blocks(0, 0, 3)
+    mine = pltpu.make_async_copy(hid, hid_out.at[l], ls.at[4])
+    mine.start()
     cc.append(gr_other(1, yr))
     cc.append(gr_other(2, yl))
     gr_own(0, 1, yr)

time: 145 us -> 137 us (0.945)
  Pallas kernels: 142 us -> 134 us
    pallas_call x1, Pallas kernels: 137 us -> 129 us  [fused(): pl.pallas_call(kernel, out_shape=(jax.ShapeDtypeStruct((2, 2, 4, BLOCK, T...]
where the time goes in v8:
time: 137 us; the launch traced here: 136 us
  Pallas kernels  134 us (98%)
  local copies, waits for them, and re-layouts  1.92 us (1%)
    pallas_call x1, Pallas kernels, fused(): pl.pallas_call(kernel, out_shape=(jax.ShapeDtypeStruct((2, 2, 4, BLOCK, T...  129 us
    pallas_call x1, Pallas kernels, merge(): pl.pallas_call(merge_kernel, out_shape=jax.ShapeDtypeStruct((FF_TILE, TOK...  4.57 us

profile of v8, /device:TPU:0, one launch (start us, length us, event | category | flops | bytes accessed | tf_op | source)
XLA Modules:
  0.0 136.2 jit_solution(8784507870925340247)
XLA Ops:
  0.6 129.1 %swiglu_grid.1 = (bf16[2,2,4,112,1024]{4,3,2,1,0:T(8,128)(2,1)}, bf16[256,1280]{1,0:T(8,128)(2,1)}, f32[2,112,1280]{2,1,0:T(8,128)}) custom-call(bf16[256,1280]{1,0:T(8,128)(2,1)} %tok_ref.1, bf16[108,1280]{1,0:T(8,128)(2,1)} %gw_ref.1, bf16[108,1280]{1,0:T(8,128)(2,1)} %uw_ref.1, bf16[1728,1024]{1,0:T(8,128)(2,1)} %bitcast.7), custom_call_target="tpu_custom_call" | custom-call | flops 28185722880 | bytes 12582912 | tf_op jit(solution)/shard_map/swiglu_grid/pallas_call | solution.py:549
  129.7 0.0 copy-start
  129.8 0.0 copy-start.1
  129.8 4.6 %merge_hidden.1 = bf16[1728,1024]{1,0:T(8,128)(2,1)} custom-call(bf16[2,2,4,112,1024]{4,3,2,1,0:T(8,128)(2,1)} %get-tuple-element.7.hid_ref), custom_call_target="tpu_custom_call" | custom-call | tf_op jit(solution)/shard_map/merge_hidden/pallas_call | solution.py:602
  134.3 0.0 copy-done
  134.3 1.1 slice_bitcast_fusion
  135.4 0.0 copy-done.1
  135.4 0.8 copy.9
Async XLA Ops:
  129.7 4.6 %copy-start = (f32[2,112,1280]{2,1,0:T(8,128)S(1)}, f32[2,112,1280]{2,1,0:T(8,128)}, u32[]{:S(2)}) copy-start(f32[2,112,1280]{2,1,0:T(8,128)} %get-tuple-element.9) | copy-start | bytes 3440644
  129.8 5.7 %copy-start.1 = (bf16[256,1280]{1,0:T(8,128)(2,1)S(1)}, bf16[256,1280]{1,0:T(8,128)(2,1)}, u32[]{:S(2)}) copy-start(bf16[256,1280]{1,0:T(8,128)(2,1)} %get-tuple-element.17) | copy-start | bytes 1966084

commit v9 on v8

--- a/solution.py
+++ b/solution.py
@@ -440,34 +440,37 @@
     mine.start()
     cc.append(gr_other(1, yr))
     cc.append(gr_other(2, yl))
-    gr_own(0, 1, yr)
-    gr_own(1, 2, yl)
     of_j = (1 - h, h)
     y2 = []
-    for d, (at, to) in enumerate(((Y2R, y_right), (Y2L, y_left))):
+    for d, (yy, at, to) in enumerate(((yr, Y2R, y_right), (yl, Y2L, y_left))):
+        part = gr_sums(1 + d, yy)
+        for hh in range(2):
+            for m in range(2):
+                if m == d:
+                    continue
+                own[d, hh, m] = part(hh, m)
         y1[d].wait_recv()
+        for hh in range(2):
+            own[d, hh, d] = part(hh, d) + y1r[d, hh].astype(F32)
         y2.append([])
         for j, hh in enumerate(of_j):
             for m in range(2):
-                total = own[d, hh, m]
-                if m == d:
-                    total = total + y1r[d, hh].astype(F32)
-                y2s[d, j, m] = total.astype(BF)
+                y2s[d, j, m] = own[d, hh, m].astype(BF)
                 cp = remote(y2s.at[d, j, m], y2r.at[d, j, m], at + 2 * j + m, to)
                 if j == 0:
                     cp.start()
                 y2[d].append(cp)
     tg_near(1)
     mine_other = tg_rows(z, 0)
+    cc.append(gr_other(3, y))
     g2[0].wait_recv()
     g2[1].wait_recv()
     txs[...] = (mine_other + tgr2[0, 0].astype(F32) + tgr2[1, 0].astype(F32)).astype(BF)
     gx = send(txs, txr, GX, x_peer)
-    cc.append(gr_other(3, y))
-    tgo[...] = tg_rows(z, 1)
     for d in range(2):
         g2[d].wait_send()
         g2[2 + d].start()
+    tgo[...] = tg_rows(z, 1)
     gr_own(0, 3, y)
 
     def next_piece(m, before):
@@ -602,9 +605,9 @@
     return pl.pallas_call(
         merge_kernel,
         out_shape=jax.ShapeDtypeStruct((FF_TILE, TOK), BF),
-        grid=(4,),
-        in_specs=[pl.BlockSpec((2, 2, 1, BLOCK, TOK), lambda i: (0, 0, i, 0, 0))],
-        out_specs=pl.BlockSpec((4 * SHARD, TOK), lambda i: (i, 0)),
+        grid=(4, 2),
+        in_specs=[pl.BlockSpec((2, 2, 1, BLOCK, TOK // 2), lambda i, j: (0, 0, i, 0, j))],
+        out_specs=pl.BlockSpec((4 * SHARD, TOK // 2), lambda i, j: (i, j)),
         name="merge_hidden",
     )(hid)
 

time: 137 us -> 140 us (1.022)
  Pallas kernels: 134 us -> 137 us
    pallas_call x1, Pallas kernels: 4.57 us -> 6.53 us  [merge(): pl.pallas_call(merge_kernel, out_shape=jax.ShapeDtypeStruct((FF_TILE, TOK...]
where the time goes in v9:
time: 140 us; the launch traced here: 139 us
  Pallas kernels  137 us (98%)
  local copies, waits for them, and re-layouts  1.92 us (1%)
    pallas_call x1, Pallas kernels, fused(): pl.pallas_call(kernel, out_shape=(jax.ShapeDtypeStruct((2, 2, 4, BLOCK, T...  130 us
    pallas_call x1, Pallas kernels, merge(): pl.pallas_call(merge_kernel, out_shape=jax.ShapeDtypeStruct((FF_TILE, TOK...  6.53 us

profile of v9, /device:TPU:0, one launch (start us, length us, event | category | flops | bytes accessed | tf_op | source)
XLA Modules:
  0.0 139.3 jit_solution(5793211397166948870)
XLA Ops:
  0.6 130.2 %swiglu_grid.1 = (bf16[2,2,4,112,1024]{4,3,2,1,0:T(8,128)(2,1)}, bf16[256,1280]{1,0:T(8,128)(2,1)}, f32[2,112,1280]{2,1,0:T(8,128)}) custom-call(bf16[256,1280]{1,0:T(8,128)(2,1)} %tok_ref.1, bf16[108,1280]{1,0:T(8,128)(2,1)} %gw_ref.1, bf16[108,1280]{1,0:T(8,128)(2,1)} %uw_ref.1, bf16[1728,1024]{1,0:T(8,128)(2,1)} %bitcast.7), custom_call_target="tpu_custom_call" | custom-call | flops 28185722880 | bytes 12582912 | tf_op jit(solution)/shard_map/swiglu_grid/pallas_call | solution.py:552
  130.9 0.0 copy-start
  130.9 0.0 copy-start.1
  130.9 6.5 %merge_hidden.1 = bf16[1728,1024]{1,0:T(8,128)(2,1)} custom-call(bf16[2,2,4,112,1024]{4,3,2,1,0:T(8,128)(2,1)} %get-tuple-element.7.hid_ref), custom_call_target="tpu_custom_call" | custom-call | tf_op jit(solution)/shard_map/merge_hidden/pallas_call | solution.py:605
  137.4 0.0 copy-done
  137.4 1.1 slice_bitcast_fusion
  138.5 0.0 copy-done.1
  138.5 0.8 copy.9
Async XLA Ops:
  130.9 6.6 %copy-start = (f32[2,112,1280]{2,1,0:T(8,128)S(1)}, f32[2,112,1280]{2,1,0:T(8,128)}, u32[]{:S(2)}) copy-start(f32[2,112,1280]{2,1,0:T(8,128)} %get-tuple-element.9) | copy-start | bytes 3440644
  130.9 7.6 %copy-start.1 = (bf16[256,1280]{1,0:T(8,128)(2,1)S(1)}, bf16[256,1280]{1,0:T(8,128)(2,1)}, u32[]{:S(2)}) copy-start(bf16[256,1280]{1,0:T(8,128)(2,1)} %get-tuple-element.17) | copy-start | bytes 1966084

commit v10 on v9

--- a/solution.py
+++ b/solution.py
@@ -597,17 +597,18 @@
 
 
 def merge_kernel(hid_ref, out_ref):
-    parts = [hid_ref[side, hh, 0, :SHARD] for hh in range(2) for side in range(2)]
-    out_ref[...] = jnp.concatenate(parts, axis=0)
+    for at in range(2):
+        parts = [hid_ref[side, hh, at, :SHARD] for hh in range(2) for side in range(2)]
+        out_ref[pl.ds(at * 4 * SHARD, 4 * SHARD), :] = jnp.concatenate(parts, axis=0)
 
 
 def merge(hid):
     return pl.pallas_call(
         merge_kernel,
         out_shape=jax.ShapeDtypeStruct((FF_TILE, TOK), BF),
-        grid=(4, 2),
-        in_specs=[pl.BlockSpec((2, 2, 1, BLOCK, TOK // 2), lambda i, j: (0, 0, i, 0, j))],
-        out_specs=pl.BlockSpec((4 * SHARD, TOK // 2), lambda i, j: (i, j)),
+        grid=(2,),
+        in_specs=[pl.BlockSpec((2, 2, 2, BLOCK, TOK), lambda i: (0, 0, i, 0, 0))],
+        out_specs=pl.BlockSpec((8 * SHARD, TOK), lambda i: (i, 0)),
         name="merge_hidden",
     )(hid)
 

time: 140 us -> 137 us (0.979)
  Pallas kernels: 137 us -> 134 us
    pallas_call x1, Pallas kernels: 6.53 us -> 3.58 us  [merge(): pl.pallas_call(merge_kernel, out_shape=jax.ShapeDtypeStruct((FF_TILE, TOK...]
where the time goes in v10:
time: 137 us; the launch traced here: 136 us
  Pallas kernels  134 us (98%)
  local copies, waits for them, and re-layouts  1.92 us (1%)
    pallas_call x1, Pallas kernels, fused(): pl.pallas_call(kernel, out_shape=(jax.ShapeDtypeStruct((2, 2, 4, BLOCK, T...  130 us
    pallas_call x1, Pallas kernels, merge(): pl.pallas_call(merge_kernel, out_shape=jax.ShapeDtypeStruct((FF_TILE, TOK...  3.58 us

profile of v10, /device:TPU:0, one launch (start us, length us, event | category | flops | bytes accessed | tf_op | source)
XLA Modules:
  0.0 136.4 jit_solution(18427413959726867373)
XLA Ops:
  0.6 130.2 %swiglu_grid.1 = (bf16[2,2,4,112,1024]{4,3,2,1,0:T(8,128)(2,1)}, bf16[256,1280]{1,0:T(8,128)(2,1)}, f32[2,112,1280]{2,1,0:T(8,128)}) custom-call(bf16[256,1280]{1,0:T(8,128)(2,1)} %tok_ref.1, bf16[108,1280]{1,0:T(8,128)(2,1)} %gw_ref.1, bf16[108,1280]{1,0:T(8,128)(2,1)} %uw_ref.1, bf16[1728,1024]{1,0:T(8,128)(2,1)} %bitcast.7), custom_call_target="tpu_custom_call" | custom-call | flops 28185722880 | bytes 12582912 | tf_op jit(solution)/shard_map/swiglu_grid/pallas_call | solution.py:552
  130.9 0.0 copy-start
  130.9 0.0 copy-start.1
  130.9 3.6 %merge_hidden.1 = bf16[1728,1024]{1,0:T(8,128)(2,1)} custom-call(bf16[2,2,4,112,1024]{4,3,2,1,0:T(8,128)(2,1)} %get-tuple-element.7.hid_ref), custom_call_target="tpu_custom_call" | custom-call | tf_op jit(solution)/shard_map/merge_hidden/pallas_call | solution.py:606
  134.5 0.0 copy-done
  134.5 1.1 slice_bitcast_fusion
  135.5 0.0 copy-done.1
  135.5 0.8 copy.9
Async XLA Ops:
  130.9 3.6 %copy-start = (f32[2,112,1280]{2,1,0:T(8,128)S(1)}, f32[2,112,1280]{2,1,0:T(8,128)}, u32[]{:S(2)}) copy-start(f32[2,112,1280]{2,1,0:T(8,128)} %get-tuple-element.9) | copy-start | bytes 3440644
  130.9 4.7 %copy-start.1 = (bf16[256,1280]{1,0:T(8,128)(2,1)S(1)}, bf16[256,1280]{1,0:T(8,128)(2,1)}, u32[]{:S(2)}) copy-start(bf16[256,1280]{1,0:T(8,128)(2,1)} %get-tuple-element.17) | copy-start | bytes 1966084
